TPU v7x, 32 devices: a whole 2x2x4 slice. The times are simulated.
32 devices in a mesh: groups: 2 (over y), rows: 4 (over z), section: 4 (over x, core).
Axes of the slice: x: 2, y: 2, z: 4, core: 2. Of those that a mesh axis runs over, the one named last changes fastest.
Arguments:
- latent: bfloat16 [8, 16, 16, 768], P('groups', 'rows'), parts along dimension 0, may hold values from -1000 to 1000
- target: bfloat16 [8, 16, 16, 768], P('groups', 'rows'), parts along dimension 0, may hold values from -60 to 60
- expand_weight: bfloat16 [4, 768, 1536], P('section', 'rows'), may hold values from -0.21875 to 0.21875
- expand_bias: float32 [4, 1536], P('section'), may hold values from -2 to 2
- reduce_weight: bfloat16 [4, 1536, 768], P('section', 'rows'), may hold values from -0.15625 to 0.15625
- reduce_bias: float32 [4, 768], P('section'), may hold values from -2 to 2
- depth_kernel: float32 [4, 49, 768], P('section'), may hold values from -0.8 to 0.8
- depth_offset: float32 [4, 768], P('section'), may hold values from -2 to 2
- norm_gain: float32 [4, 768], P('section'), may hold values from 0.1 to 1.9
- norm_shift: float32 [4, 768], P('section'), may hold values from -1.2 to 1.2
- layer_scale: float32 [4, 768], P('section'), may hold values from 0.2 to 0.6
Outputs:
- kernel_gradient: float32 [8, 49, 768], P(('groups', 'section')), parts along dimension 0
- offset_gradient: float32 [8, 768], P(('groups', 'section')), parts along dimension 0
- gain_gradient: float32 [8, 768], P(('groups', 'section')), parts along dimension 0
- shift_gradient: float32 [8, 768], P(('groups', 'section')), parts along dimension 0
- scale_gradient: float32 [8, 768], P(('groups', 'section')), parts along dimension 0
There are 2 independent parts, one for each index of `groups`. A program takes and returns all parts, laid end to end along the dimension named above; an argument that names none is the same for every part. Nothing has to cross between parts.
All inputs are finite; a program needn't handle non-finite values.
Results may differ from a plain program's by a relative error of at most 0.005.
The roundings to bfloat16 on the way count: a program that leaves them out, or rounds other values in their place, can miss the bound.
Values may be sent and summed in bfloat16 or wider, within the bound.
A program may use at most 64 MiB of HBM per device.

v0:
```python
import math

import jax
import jax.numpy as jnp
from jax import lax
from jax.sharding import PartitionSpec as P

KS = 7


EPSILON = 1e-06
SQRT_HALF = 0.7071067811865476
INV_ROOT_TAU = 0.3989422804014327


def shifted(value, axis, steps):
    count = lax.axis_size(axis)
    first, last = (max(0, -steps), min(count, count - steps))
    return lax.ppermute(value, axis, [(source, source + steps) for source in range(first, last)])


def with_halo(block, sides, width):
    for axis, dim in sides:
        count = lax.axis_size(axis)
        forward = [(i, i + 1) for i in range(count - 1)]
        backward = [(target, source) for source, target in forward]
        low = lax.ppermute(
            lax.slice_in_dim(block, block.shape[dim] - width, None, axis=dim), axis, forward
        )
        high = lax.ppermute(lax.slice_in_dim(block, 0, width, axis=dim), axis, backward)
        block = jnp.concatenate([low, block, high], axis=dim)
    return block


def depthwise(padded, kernel, offset, height, breadth):
    summed = jnp.zeros((height, breadth, padded.shape[2]), jnp.float32) + offset
    for row_off in range(KS):
        for col_off in range(KS):
            summed = (
                summed
                + kernel[row_off * KS + col_off]
                * padded[row_off : row_off + height, col_off : col_off + breadth]
            )
    return summed


def depthwise_back(padded_slope, kernel, height, breadth):
    margin = KS // 2
    wide_slope = padded_slope.astype(jnp.float32)
    summed = jnp.zeros((height, breadth, padded_slope.shape[2]), jnp.float32)
    for row_off in range(KS):
        for col_off in range(KS):
            first_row = 2 * margin - row_off
            first_col = 2 * margin - col_off
            summed = (
                summed
                + kernel[row_off * KS + col_off]
                * wide_slope[first_row : first_row + height, first_col : first_col + breadth]
            )
    return summed


def kernel_terms(padded, slope, height, breadth):
    pieces = []
    for row_off in range(KS):
        for col_off in range(KS):
            pieces.append(
                jnp.sum(
                    slope * padded[row_off : row_off + height, col_off : col_off + breadth],
                    axis=(0, 1),
                )
            )
    return jnp.stack(pieces)


def normalize(flat):
    centre = jnp.mean(flat, axis=-1, keepdims=True)
    centred = flat - centre
    variance = jnp.mean(centred * centred, axis=-1, keepdims=True)
    inverse = lax.rsqrt(variance + EPSILON)
    return (centred * inverse, inverse)


def gelu_slope(hidden):
    return (
        0.5 * (1.0 + jax.scipy.special.erf(hidden * SQRT_HALF))
        + hidden * jnp.exp(-0.5 * hidden * hidden) * INV_ROOT_TAU
    )


def contract_last(left, right):
    return lax.dot_general(
        left, right, (((1,), (1,)), ((), ())), preferred_element_type=jnp.float32
    )


def project_forward(mixed, gain, shift, w_expand, b_expand, w_reduce, b_reduce):
    normed, inverse = normalize(mixed)
    inputs = (normed * gain + shift).astype(jnp.bfloat16)
    hidden = jnp.dot(inputs, w_expand, preferred_element_type=jnp.float32) + b_expand
    active = jax.nn.gelu(hidden, approximate=False).astype(jnp.bfloat16)
    branch = jnp.dot(active, w_reduce, preferred_element_type=jnp.float32) + b_reduce
    return (normed, inverse, hidden, branch)


def project_backward(incoming, normed, inverse, hidden, branch, gain, scale, w_expand, w_reduce):
    arrived = incoming.astype(jnp.float32)
    scale_term = jnp.sum(arrived * branch, axis=0)
    reduced = (arrived * scale).astype(jnp.bfloat16)
    spread = contract_last(reduced, w_reduce)
    hidden_slope = (spread * gelu_slope(hidden)).astype(jnp.bfloat16)
    normal_slope = contract_last(hidden_slope, w_expand)
    gain_term = jnp.sum(normal_slope * normed, axis=0)
    shift_term = jnp.sum(normal_slope, axis=0)
    scaled = normal_slope * gain
    slope = (
        scaled
        - jnp.mean(scaled, axis=-1, keepdims=True)
        - normed * jnp.mean(scaled * normed, axis=-1, keepdims=True)
    ) * inverse
    offset_term = jnp.sum(slope, axis=0)
    return (slope, scale_term, gain_term, shift_term, offset_term)


def per_device(
    latent,
    target,
    expand_weight,
    expand_bias,
    reduce_weight,
    reduce_bias,
    depth_kernel,
    depth_offset,
    norm_gain,
    norm_shift,
    layer_scale,
):
    sections = lax.axis_size("section")
    section_pos = lax.axis_index("section")
    micro_count, height, breadth, channels = latent.shape
    margin = KS // 2
    moments = micro_count + sections - 1
    total_rows = height * lax.axis_size("rows")
    loss_scale = 1.0 / math.sqrt(micro_count * total_rows * breadth)
    kernel = depth_kernel[0]
    offset = depth_offset[0]
    gain = norm_gain[0]
    shift = norm_shift[0]
    scale = layer_scale[0]
    b_expand = expand_bias[0]
    b_reduce = reduce_bias[0]
    hidden_units = expand_weight.shape[2]
    tokens = height * breadth
    w_expand, w_reduce = (
        lax.all_gather(expand_weight[0], "rows", axis=0, tiled=True),
        lax.all_gather(reduce_weight[0], "rows", axis=0, tiled=True),
    )
    spare_grid = jnp.zeros((height, breadth, channels), jnp.bfloat16)
    kept = (
        jnp.zeros((micro_count, height + 2 * margin, breadth, channels), jnp.bfloat16),
        jnp.zeros((micro_count, tokens, channels), jnp.float32),
        jnp.zeros((micro_count, height, breadth, channels), jnp.bfloat16),
    )
    kept = kept + (
        jnp.zeros((micro_count, tokens, hidden_units), jnp.float32),
        jnp.zeros((micro_count, tokens, channels), jnp.float32),
    )

    def forward_moment(state_in, moment):
        previous, stores = state_in
        arrived = shifted(previous, "section", 1)
        micro_pos = moment - section_pos
        valid = (micro_pos >= 0) & (micro_pos < micro_count)
        safe_pos = jnp.clip(micro_pos, 0, micro_count - 1)
        fresh = lax.dynamic_index_in_dim(latent, safe_pos, 0, keepdims=False)
        source = jnp.where(section_pos == 0, fresh, arrived)
        framed = with_halo(source, (("rows", 0),), margin)

        def forward_working(buffers):
            padded = jnp.pad(framed.astype(jnp.float32), ((0, 0), (margin, margin), (0, 0)))
            mixed = depthwise(padded, kernel, offset, height, breadth).reshape(tokens, channels)
            normed, inverse, hidden, branch = project_forward(
                mixed, gain, shift, w_expand, b_expand, w_reduce, b_reduce
            )
            output = (
                source.astype(jnp.float32) + scale * branch.reshape(height, breadth, channels)
            ).astype(jnp.bfloat16)
            fresh_items = (framed, mixed, output)
            fresh_items = fresh_items + (hidden, branch)
            updated = tuple(
                (
                    lax.dynamic_update_index_in_dim(buffer, element, safe_pos, 0)
                    for buffer, element in zip(buffers, fresh_items)
                )
            )
            return (output, updated)

        def forward_resting(buffers):
            return (spare_grid, buffers)

        output, stores = lax.cond(valid, forward_working, forward_resting, stores)
        return ((output, stores), None)

    forward_state = lax.scan(forward_moment, (spare_grid, kept), jnp.arange(moments))[0]
    kept = forward_state[1]
    back_expand, back_reduce = (
        lax.all_gather(expand_weight[0], "rows", axis=0, tiled=True),
        lax.all_gather(reduce_weight[0], "rows", axis=0, tiled=True),
    )
    zero_sums = (
        jnp.zeros((KS * KS, channels), jnp.float32),
        jnp.zeros((channels,), jnp.float32),
        jnp.zeros((channels,), jnp.float32),
        jnp.zeros((channels,), jnp.float32),
        jnp.zeros((channels,), jnp.float32),
    )

    def backward_moment(state_in, moment):
        previous, totals = state_in
        arrived = shifted(previous, "section", -1)
        micro_pos = moment - (sections - 1 - section_pos)
        valid = (micro_pos >= 0) & (micro_pos < micro_count)
        safe_pos = jnp.clip(micro_pos, 0, micro_count - 1)
        own_output = lax.dynamic_index_in_dim(kept[2], safe_pos, 0, keepdims=False)
        aimed = lax.dynamic_index_in_dim(target, safe_pos, 0, keepdims=False)
        start_slope = (
            (own_output.astype(jnp.float32) - aimed.astype(jnp.float32)) * loss_scale
        ).astype(jnp.bfloat16)
        incoming = jnp.where(section_pos == sections - 1, start_slope, arrived)

        def backward_working(running):
            framed = lax.dynamic_index_in_dim(kept[0], safe_pos, 0, keepdims=False)
            mixed = lax.dynamic_index_in_dim(kept[1], safe_pos, 0, keepdims=False)
            normed, inverse = normalize(mixed)
            hidden = lax.dynamic_index_in_dim(kept[3], safe_pos, 0, keepdims=False)
            branch = lax.dynamic_index_in_dim(kept[4], safe_pos, 0, keepdims=False)
            slope, scale_term, gain_term, shift_term, offset_term = project_backward(
                incoming.reshape(tokens, channels),
                normed,
                inverse,
                hidden,
                branch,
                gain,
                scale,
                back_expand,
                back_reduce,
            )
            padded = jnp.pad(framed.astype(jnp.float32), ((0, 0), (margin, margin), (0, 0)))
            slope_grid = slope.reshape(height, breadth, channels)
            kernel_term = kernel_terms(padded, slope_grid, height, breadth)
            new_totals = (
                running[0] + kernel_term,
                running[1] + offset_term,
                running[2] + gain_term,
                running[3] + shift_term,
                running[4] + scale_term,
            )
            return (slope_grid.astype(jnp.bfloat16), new_totals)

        def backward_resting(running):
            return (spare_grid, running)

        slope_low, totals = lax.cond(valid, backward_working, backward_resting, totals)
        slope_framed = with_halo(slope_low, (("rows", 0),), margin)
        padded_slope = jnp.pad(slope_framed, ((0, 0), (margin, margin), (0, 0)))
        spread_back = depthwise_back(padded_slope, kernel, height, breadth)
        passed = (incoming.astype(jnp.float32) + spread_back).astype(jnp.bfloat16)
        passed = jnp.where(valid, passed, spare_grid)
        return ((passed, totals), None)

    backward_state = lax.scan(backward_moment, (spare_grid, zero_sums), jnp.arange(moments))[0]
    totals = backward_state[1]
    kernel_sum, offset_sum, gain_sum, shift_sum, scale_sum = lax.psum(
        (totals[0], totals[1], totals[2], totals[3], totals[4]), "rows"
    )
    return (kernel_sum[None], offset_sum[None], gain_sum[None], shift_sum[None], scale_sum[None])


def solution(mesh):
    placed = (
        P("groups", "rows", None, None),
        P("groups", "rows", None, None),
        P("section", "rows", None),
        P("section", None),
        P("section", "rows", None),
        P("section", None),
        P("section", None, None),
        P("section", None),
        P("section", None),
        P("section", None),
        P("section", None),
    )
    return jax.shard_map(
        per_device,
        mesh=mesh,
        in_specs=placed,
        out_specs=(
            P(("groups", "section"), None, None),
            P(("groups", "section"), None),
            P(("groups", "section"), None),
            P(("groups", "section"), None),
            P(("groups", "section"), None),
        ),
        check_vma=False,
    )
```

profile of v0, /device:TPU:0, one launch (start us, length us, event | category | flops | bytes accessed | tf_op | source)
XLA Modules:
  0.0 587.9 jit_solution(4347107190480502940)
XLA Ops:
  10.3 52.5 %all-gather.5.cloned.1.call-done = bf16[1,768,1536]{2,1,0:T(8,128)(2,1)} async-done(((bf16[1,192,1536]{2,1,0:T(8,128)(2,1)}), bf16[1,768,1536]{2,1,0:T(8,128)(2,1)}) %all-gather.5.cloned.1.call-update) | async-done | bytes 2359312 | tf_op jit(solution)/shard_map/all_gather | solution.py:155
  62.8 50.9 %all-gather.7.cloned.1.call-done = bf16[1,1536,768]{2,1,0:T(8,128)(2,1)} async-done(((bf16[1,384,768]{2,1,0:T(8,128)(2,1)}), bf16[1,1536,768]{2,1,0:T(8,128)(2,1)}) %all-gather.7.cloned.1.call-update) | async-done | bytes 2359312 | tf_op jit(solution)/shard_map/all_gather | solution.py:156
  120.1 195.3 %while.44 = (s32[]{:T(128)}, bf16[4,16,768]{2,1,0:T(8,128)(2,1)}, bf16[4,10,16,768]{3,2,1,0:T(8,128)(2,1)}, f32[4,64,768]{2,1,0:T(8,128)}, bf16[4,4,16,768]{3,2,...) while((s32[]{:T(128)}, bf16[4,16,768]{2,1,0:T(8,128)(2,1)}, ...), condition=%wide.region_5.6_spmd, body=%wide.region_0.5_spmd.sunk | while | flops 314400832 | bytes 13684738 | solution.py:204
  120.1 1.7 collective-permute-start
  125.9 4.5 collective-permute-start.2
  130.8 1.6 collective-permute-done.2
  132.5 20.0 %conditional.5 = (bf16[4,16,768]{2,1,0:T(8,128)(2,1)}, bf16[4,10,16,768]{3,2,1,0:T(8,128)(2,1)}, f32[4,64,768]{2,1,0:T(8,128)}, bf16[4,4,16,768]{3,2,1,0:T(8,128...) conditional(s32[]{:T(128)} %convert_element_type.155, (bf16[4,10,16,768]{3,2,1,0:T(8,128)(2,1)}, ...), branch_computations={%region_1.1_spmd, %region_2.4_spmd} | conditional | flops 314105920 | bytes 11619766 | solution.py:201
  132.5 2.1 slice_reduce_fusion.48
  134.6 2.1 slice_reduce_fusion.47
  136.7 1.8 slice_reduce_fusion.46
  139.8 2.1 fusion.355
  145.9 3.6 bitcast_dynamic-update-slice_fusion.2
  149.5 1.6 bitcast_dynamic-update-slice_fusion.4
  157.9 5.0 collective-permute-start.2
  164.9 20.1 %conditional.5 = (bf16[4,16,768]{2,1,0:T(8,128)(2,1)}, bf16[4,10,16,768]{3,2,1,0:T(8,128)(2,1)}, f32[4,64,768]{2,1,0:T(8,128)}, bf16[4,4,16,768]{3,2,1,0:T(8,128...) conditional(s32[]{:T(128)} %convert_element_type.155, (bf16[4,10,16,768]{3,2,1,0:T(8,128)(2,1)}, ...), branch_computations={%region_1.1_spmd, %region_2.4_spmd} | conditional | flops 314105920 | bytes 11619766 | solution.py:201
  164.9 2.1 slice_reduce_fusion.48
  167.0 2.1 slice_reduce_fusion.47
  169.1 1.8 slice_reduce_fusion.46
  172.2 2.1 fusion.355
  178.3 3.7 bitcast_dynamic-update-slice_fusion.2
  181.9 1.6 bitcast_dynamic-update-slice_fusion.4
  190.3 4.9 collective-permute-start.2
  197.2 20.0 %conditional.5 = (bf16[4,16,768]{2,1,0:T(8,128)(2,1)}, bf16[4,10,16,768]{3,2,1,0:T(8,128)(2,1)}, f32[4,64,768]{2,1,0:T(8,128)}, bf16[4,4,16,768]{3,2,1,0:T(8,128...) conditional(s32[]{:T(128)} %convert_element_type.155, (bf16[4,10,16,768]{3,2,1,0:T(8,128)(2,1)}, ...), branch_computations={%region_1.1_spmd, %region_2.4_spmd} | conditional | flops 314105920 | bytes 11619766 | solution.py:201
  197.2 2.1 slice_reduce_fusion.48
  199.3 2.1 slice_reduce_fusion.47
  201.4 1.8 slice_reduce_fusion.46
  204.5 2.1 fusion.355
  210.6 3.6 bitcast_dynamic-update-slice_fusion.2
  214.2 1.6 bitcast_dynamic-update-slice_fusion.4
  222.6 4.9 collective-permute-start.2
  229.5 20.0 %conditional.5 = (bf16[4,16,768]{2,1,0:T(8,128)(2,1)}, bf16[4,10,16,768]{3,2,1,0:T(8,128)(2,1)}, f32[4,64,768]{2,1,0:T(8,128)}, bf16[4,4,16,768]{3,2,1,0:T(8,128...) conditional(s32[]{:T(128)} %convert_element_type.155, (bf16[4,10,16,768]{3,2,1,0:T(8,128)(2,1)}, ...), branch_computations={%region_1.1_spmd, %region_2.4_spmd} | conditional | flops 314105920 | bytes 11619766 | solution.py:201
  229.5 2.1 slice_reduce_fusion.48
  231.6 2.1 slice_reduce_fusion.47
  233.7 1.8 slice_reduce_fusion.46
  236.8 2.1 fusion.355
  242.8 3.6 bitcast_dynamic-update-slice_fusion.2
  246.5 1.6 bitcast_dynamic-update-slice_fusion.4
  249.5 3.3 collective-permute-start
  256.9 4.6 collective-permute-start.2
  264.2 24.0 %collective-permute-start = (bf16[4,16,768]{2,1,0:T(8,128)(2,1)}, bf16[4,16,768]{2,1,0:T(8,128)(2,1)S(1)}, u32[]{:S(2)}, u32[]{:S(2)}) collective-permute-start(bf16[4,16,768]{2,1,0:T(8,128)(2,1)} %get-tuple-element.1363), channel_id=1, source_target_pairs={{0,1},{1,2},{2,3},{4,5},{5,6},{6,7},{8,9},{9,10},{10,11},{12,13},{... | collective-permute-start | bytes 294920 | tf_op jit(solution)/shard_map/while/body/eval_jaxpr/ppermute | solution.py:19
  292.2 4.6 collective-permute-start.2
  299.5 4.6 collective-permute-start
  308.2 4.6 collective-permute-start.2
  315.5 227.0 %while.45 = (s32[]{:T(128)}, bf16[4,16,768]{2,1,0:T(8,128)(2,1)S(1)}, f32[49,768]{1,0:T(8,128)S(1)}, f32[768]{0:T(1024)S(1)}, f32[768]{0:T(1024)S(1)}, /*index=5...) while((s32[]{:T(128)}, ...), condition=%wide.region_66.67_spmd.clone, body=%wide.region_6.66_spmd.clone.sunk | while | flops 316624960 | bytes 26198456 | solution.py:271
  321.0 19.3 %collective-permute-done.3 = bf16[4,16,768]{2,1,0:T(8,128)(2,1)S(1)} collective-permute-done((bf16[4,16,768]{2,1,0:T(8,128)(2,1)S(1)}, bf16[4,16,768]{2,1,0:T(8,128)(2,1)S(1)}, u32[]{:S(2)}, u32[]{:S(2)}) %collective-permute-start.3) | collective-permute-done | bytes 98336 | tf_op jit(solution)/shard_map/while/body/eval_jaxpr/ppermute | solution.py:19
  342.7 4.6 collective-permute-start.5
  359.8 4.6 collective-permute-start.5
  373.2 12.3 %collective-permute-done.3 = bf16[4,16,768]{2,1,0:T(8,128)(2,1)S(1)} collective-permute-done((bf16[4,16,768]{2,1,0:T(8,128)(2,1)S(1)}, bf16[4,16,768]{2,1,0:T(8,128)(2,1)S(1)}, u32[]{:S(2)}, u32[]{:S(2)}) %collective-permute-start.3) | collective-permute-done | bytes 98336 | tf_op jit(solution)/shard_map/while/body/eval_jaxpr/ppermute | solution.py:19
  387.9 4.6 collective-permute-start.5
  401.4 33.9 %collective-permute-done.3 = bf16[4,16,768]{2,1,0:T(8,128)(2,1)S(1)} collective-permute-done((bf16[4,16,768]{2,1,0:T(8,128)(2,1)S(1)}, bf16[4,16,768]{2,1,0:T(8,128)(2,1)S(1)}, u32[]{:S(2)}, u32[]{:S(2)}) %collective-permute-start.3) | collective-permute-done | bytes 98336 | tf_op jit(solution)/shard_map/while/body/eval_jaxpr/ppermute | solution.py:19
  436.2 11.6 %conditional.6 = (bf16[4,16,768]{2,1,0:T(8,128)(2,1)S(1)}, f32[49,768]{1,0:T(8,128)S(1)}, f32[768]{0:T(1024)S(1)}, f32[768]{0:T(1024)S(1)}, f32[768]{0:T(1024)S(1)}, /*index=5*/f32[768]{0:T(1024)S(1)}) conditional(s32[]{:T(128)} %convert_element_type.162, (f32[49,768]{1,0:T(8,128)S(1)}, f32[768]{0:T(1024)S(1)}, f32[768]{0:T(1024)S(1)}, ...), branch_computations={%region_7.7_spmd, %region_8.65_spmd} | conditional | flops 309289024 | bytes 13126506 | solution.py:263
  440.0 3.5 multiply_reduce_fusion.1
  449.2 4.6 collective-permute-start.5
  464.7 11.6 %conditional.6 = (bf16[4,16,768]{2,1,0:T(8,128)(2,1)S(1)}, f32[49,768]{1,0:T(8,128)S(1)}, f32[768]{0:T(1024)S(1)}, f32[768]{0:T(1024)S(1)}, f32[768]{0:T(1024)S(1)}, /*index=5*/f32[768]{0:T(1024)S(1)}) conditional(s32[]{:T(128)} %convert_element_type.162, (f32[49,768]{1,0:T(8,128)S(1)}, f32[768]{0:T(1024)S(1)}, f32[768]{0:T(1024)S(1)}, ...), branch_computations={%region_7.7_spmd, %region_8.65_spmd} | conditional | flops 309289024 | bytes 13126506 | solution.py:263
  468.4 3.5 multiply_reduce_fusion.1
  477.6 4.6 collective-permute-start.5
  493.3 11.6 %conditional.6 = (bf16[4,16,768]{2,1,0:T(8,128)(2,1)S(1)}, f32[49,768]{1,0:T(8,128)S(1)}, f32[768]{0:T(1024)S(1)}, f32[768]{0:T(1024)S(1)}, f32[768]{0:T(1024)S(1)}, /*index=5*/f32[768]{0:T(1024)S(1)}) conditional(s32[]{:T(128)} %convert_element_type.162, (f32[49,768]{1,0:T(8,128)S(1)}, f32[768]{0:T(1024)S(1)}, f32[768]{0:T(1024)S(1)}, ...), branch_computations={%region_7.7_spmd, %region_8.65_spmd} | conditional | flops 309289024 | bytes 13126506 | solution.py:263
  497.1 3.5 multiply_reduce_fusion.1
  506.3 4.6 collective-permute-start.5
  521.7 11.6 %conditional.6 = (bf16[4,16,768]{2,1,0:T(8,128)(2,1)S(1)}, f32[49,768]{1,0:T(8,128)S(1)}, f32[768]{0:T(1024)S(1)}, f32[768]{0:T(1024)S(1)}, f32[768]{0:T(1024)S(1)}, /*index=5*/f32[768]{0:T(1024)S(1)}) conditional(s32[]{:T(128)} %convert_element_type.162, (f32[49,768]{1,0:T(8,128)S(1)}, f32[768]{0:T(1024)S(1)}, f32[768]{0:T(1024)S(1)}, ...), branch_computations={%region_7.7_spmd, %region_8.65_spmd} | conditional | flops 309289024 | bytes 13126506 | solution.py:263
  525.4 3.5 multiply_reduce_fusion.1
  534.6 4.6 collective-permute-start.5
  543.4 21.2 %all-reduce.3 = (f32[1,768]{1,0:T(1,128)}, f32[1,768]{1,0:T(1,128)}, f32[1,768]{1,0:T(1,128)}, f32[1,768]{1,0:T(1,128)}) all-reduce(f32[1,768]{1,0:T(1,128)S(1)} %broadcast_in_dim.73, f32[1,768]{1,0:T(1,128)S(1)} %broadcast_in_dim.74, f32[1,768]{1,0:T(1,128)S(1)} %broadcast_in_dim.75, ...), channel_id=1, replica_groups=mesh['groups'=2,'rows'=4,'section'=4] {'rows'}, use_global_device_ids=true, to_apply=%region_68.69 | all-reduce | flops 3072 | bytes 24576 | tf_op jit(solution)/shard_map/psum | solution.py:273
  564.6 15.2 %all-reduce.6.cloned.1.call-done = f32[1,49,768]{2,0,1:T(1,128)} async-done(((f32[1,49,768]{2,0,1:T(1,128)}), f32[1,49,768]{2,0,1:T(1,128)}) %all-reduce.6.cloned.1.call-update) | async-done | bytes 150544 | tf_op jit(solution)/shard_map/psum | solution.py:273
  (550 shorter events, 190.6 us)
Async XLA Ops:
  7.2 55.6 %all-gather.5.cloned.1.call-start = ((), (), s32[]{:S(2)}) async-start(), calls=%async_computation.1 | async-start | bytes 2949120 | tf_op jit(solution)/shard_map/all_gather | solution.py:155
  7.9 105.8 %all-gather.7.cloned.1.call-start = ((), (), s32[]{:S(2)}) async-start(), calls=%async_computation.2 | async-start | bytes 2949120 | tf_op jit(solution)/shard_map/all_gather | solution.py:156
  8.6 571.1 %all-reduce.6.cloned.1.call-start = ((), (), s32[]{:S(2)}) async-start(), calls=%async_computation | async-start | bytes 301056 | tf_op jit(solution)/shard_map/psum | solution.py:273
  62.8 57.3 %copy-start = (bf16[1,768,1536]{2,1,0:T(8,128)(2,1)S(1)}, bf16[1,768,1536]{2,1,0:T(8,128)(2,1)}, u32[]{:S(2)}) copy-start(bf16[1,768,1536]{2,1,0:T(8,128)(2,1)} %all-gather.5.cloned.1.call-done) | copy-start | bytes 7077892
  120.1 3.5 collective-permute-start
  124.6 6.2 %collective-permute-start.1 = (bf16[3,16,768]{2,1,0:T(8,128)(2,1)S(1)}, bf16[3,16,768]{2,1,0:T(8,128)(2,1)S(1)}, u32[]{:S(2)}, u32[]{:S(2)}) collective-permute-start(bf16[3,16,768]{2,1,0:T(8,128)(2,1)S(1)} %get-tuple-element.1228), channel_id=1, source_target_pairs={{4,0},{8,4},{12,8},{5,1},{9,5},{13,9},{6,2},{10,6},{14,10},{7,3},{... | collective-permute-start | bytes 221192 | tf_op jit(solution)/shard_map/while/body/eval_jaxpr/ppermute | solution.py:30
  125.9 6.6 %collective-permute-start.2 = (bf16[3,16,768]{2,1,0:T(8,128)(2,1)S(1)}, bf16[3,16,768]{2,1,0:T(8,128)(2,1)S(1)}, u32[]{:S(2)}, u32[]{:S(2)}) collective-permute-start(bf16[3,16,768]{2,1,0:T(8,128)(2,1)S(1)} %get-tuple-element.1229), channel_id=1, source_target_pairs={{0,4},{4,8},{8,12},{1,5},{5,9},{9,13},{2,6},{6,10},{10,14},{3,7},{... | collective-permute-start | bytes 221192 | tf_op jit(solution)/shard_map/while/body/eval_jaxpr/ppermute | solution.py:27
  141.9 3.9 copy-start.2
  145.8 3.6 copy-start.1
  152.5 3.1 collective-permute-start
  156.6 6.7 %collective-permute-start.1 = (bf16[3,16,768]{2,1,0:T(8,128)(2,1)S(1)}, bf16[3,16,768]{2,1,0:T(8,128)(2,1)S(1)}, u32[]{:S(2)}, u32[]{:S(2)}) collective-permute-start(bf16[3,16,768]{2,1,0:T(8,128)(2,1)S(1)} %get-tuple-element.1228), channel_id=1, source_target_pairs={{4,0},{8,4},{12,8},{5,1},{9,5},{13,9},{6,2},{10,6},{14,10},{7,3},{... | collective-permute-start | bytes 221192 | tf_op jit(solution)/shard_map/while/body/eval_jaxpr/ppermute | solution.py:30
  157.9 7.0 %collective-permute-start.2 = (bf16[3,16,768]{2,1,0:T(8,128)(2,1)S(1)}, bf16[3,16,768]{2,1,0:T(8,128)(2,1)S(1)}, u32[]{:S(2)}, u32[]{:S(2)}) collective-permute-start(bf16[3,16,768]{2,1,0:T(8,128)(2,1)S(1)} %get-tuple-element.1229), channel_id=1, source_target_pairs={{0,4},{4,8},{8,12},{1,5},{5,9},{9,13},{2,6},{6,10},{10,14},{3,7},{... | collective-permute-start | bytes 221192 | tf_op jit(solution)/shard_map/while/body/eval_jaxpr/ppermute | solution.py:27
  174.3 3.9 copy-start.2
  178.2 3.7 copy-start.1
  185.0 3.1 collective-permute-start
  189.0 6.6 %collective-permute-start.1 = (bf16[3,16,768]{2,1,0:T(8,128)(2,1)S(1)}, bf16[3,16,768]{2,1,0:T(8,128)(2,1)S(1)}, u32[]{:S(2)}, u32[]{:S(2)}) collective-permute-start(bf16[3,16,768]{2,1,0:T(8,128)(2,1)S(1)} %get-tuple-element.1228), channel_id=1, source_target_pairs={{4,0},{8,4},{12,8},{5,1},{9,5},{13,9},{6,2},{10,6},{14,10},{7,3},{... | collective-permute-start | bytes 221192 | tf_op jit(solution)/shard_map/while/body/eval_jaxpr/ppermute | solution.py:30
  190.3 6.9 %collective-permute-start.2 = (bf16[3,16,768]{2,1,0:T(8,128)(2,1)S(1)}, bf16[3,16,768]{2,1,0:T(8,128)(2,1)S(1)}, u32[]{:S(2)}, u32[]{:S(2)}) collective-permute-start(bf16[3,16,768]{2,1,0:T(8,128)(2,1)S(1)} %get-tuple-element.1229), channel_id=1, source_target_pairs={{0,4},{4,8},{8,12},{1,5},{5,9},{9,13},{2,6},{6,10},{10,14},{3,7},{... | collective-permute-start | bytes 221192 | tf_op jit(solution)/shard_map/while/body/eval_jaxpr/ppermute | solution.py:27
  206.6 3.9 copy-start.2
  210.6 3.6 copy-start.1
  217.2 3.1 collective-permute-start
  221.3 6.6 %collective-permute-start.1 = (bf16[3,16,768]{2,1,0:T(8,128)(2,1)S(1)}, bf16[3,16,768]{2,1,0:T(8,128)(2,1)S(1)}, u32[]{:S(2)}, u32[]{:S(2)}) collective-permute-start(bf16[3,16,768]{2,1,0:T(8,128)(2,1)S(1)} %get-tuple-element.1228), channel_id=1, source_target_pairs={{4,0},{8,4},{12,8},{5,1},{9,5},{13,9},{6,2},{10,6},{14,10},{7,3},{... | collective-permute-start | bytes 221192 | tf_op jit(solution)/shard_map/while/body/eval_jaxpr/ppermute | solution.py:30
  222.6 6.9 %collective-permute-start.2 = (bf16[3,16,768]{2,1,0:T(8,128)(2,1)S(1)}, bf16[3,16,768]{2,1,0:T(8,128)(2,1)S(1)}, u32[]{:S(2)}, u32[]{:S(2)}) collective-permute-start(bf16[3,16,768]{2,1,0:T(8,128)(2,1)S(1)} %get-tuple-element.1229), channel_id=1, source_target_pairs={{0,4},{4,8},{8,12},{1,5},{5,9},{9,13},{2,6},{6,10},{10,14},{3,7},{... | collective-permute-start | bytes 221192 | tf_op jit(solution)/shard_map/while/body/eval_jaxpr/ppermute | solution.py:27
  238.9 3.9 copy-start.2
  242.8 3.6 copy-start.1
  249.5 5.2 collective-permute-start
  255.6 6.3 %collective-permute-start.1 = (bf16[3,16,768]{2,1,0:T(8,128)(2,1)S(1)}, bf16[3,16,768]{2,1,0:T(8,128)(2,1)S(1)}, u32[]{:S(2)}, u32[]{:S(2)}) collective-permute-start(bf16[3,16,768]{2,1,0:T(8,128)(2,1)S(1)} %get-tuple-element.1228), channel_id=1, source_target_pairs={{4,0},{8,4},{12,8},{5,1},{9,5},{13,9},{6,2},{10,6},{14,10},{7,3},{... | collective-permute-start | bytes 221192 | tf_op jit(solution)/shard_map/while/body/eval_jaxpr/ppermute | solution.py:30
  256.9 6.6 %collective-permute-start.2 = (bf16[3,16,768]{2,1,0:T(8,128)(2,1)S(1)}, bf16[3,16,768]{2,1,0:T(8,128)(2,1)S(1)}, u32[]{:S(2)}, u32[]{:S(2)}) collective-permute-start(bf16[3,16,768]{2,1,0:T(8,128)(2,1)S(1)} %get-tuple-element.1229), channel_id=1, source_target_pairs={{0,4},{4,8},{8,12},{1,5},{5,9},{9,13},{2,6},{6,10},{10,14},{3,7},{... | collective-permute-start | bytes 221192 | tf_op jit(solution)/shard_map/while/body/eval_jaxpr/ppermute | solution.py:27
  264.2 25.8 %collective-permute-start = (bf16[4,16,768]{2,1,0:T(8,128)(2,1)}, bf16[4,16,768]{2,1,0:T(8,128)(2,1)S(1)}, u32[]{:S(2)}, u32[]{:S(2)}) collective-permute-start(bf16[4,16,768]{2,1,0:T(8,128)(2,1)} %get-tuple-element.1363), channel_id=1, source_target_pairs={{0,1},{1,2},{2,3},{4,5},{5,6},{6,7},{8,9},{9,10},{10,11},{12,13},{... | collective-permute-start | bytes 294920 | tf_op jit(solution)/shard_map/while/body/eval_jaxpr/ppermute | solution.py:19
  290.9 6.3 %collective-permute-start.1 = (bf16[3,16,768]{2,1,0:T(8,128)(2,1)S(1)}, bf16[3,16,768]{2,1,0:T(8,128)(2,1)S(1)}, u32[]{:S(2)}, u32[]{:S(2)}) collective-permute-start(bf16[3,16,768]{2,1,0:T(8,128)(2,1)S(1)} %get-tuple-element.1228), channel_id=1, source_target_pairs={{4,0},{8,4},{12,8},{5,1},{9,5},{13,9},{6,2},{10,6},{14,10},{7,3},{... | collective-permute-start | bytes 221192 | tf_op jit(solution)/shard_map/while/body/eval_jaxpr/ppermute | solution.py:30
  292.2 6.6 %collective-permute-start.2 = (bf16[3,16,768]{2,1,0:T(8,128)(2,1)S(1)}, bf16[3,16,768]{2,1,0:T(8,128)(2,1)S(1)}, u32[]{:S(2)}, u32[]{:S(2)}) collective-permute-start(bf16[3,16,768]{2,1,0:T(8,128)(2,1)S(1)} %get-tuple-element.1229), channel_id=1, source_target_pairs={{0,4},{4,8},{8,12},{1,5},{5,9},{9,13},{2,6},{6,10},{10,14},{3,7},{... | collective-permute-start | bytes 221192 | tf_op jit(solution)/shard_map/while/body/eval_jaxpr/ppermute | solution.py:27
  299.5 6.4 %collective-permute-start = (bf16[4,16,768]{2,1,0:T(8,128)(2,1)}, bf16[4,16,768]{2,1,0:T(8,128)(2,1)S(1)}, u32[]{:S(2)}, u32[]{:S(2)}) collective-permute-start(bf16[4,16,768]{2,1,0:T(8,128)(2,1)} %get-tuple-element.1363), channel_id=1, source_target_pairs={{0,1},{1,2},{2,3},{4,5},{5,6},{6,7},{8,9},{9,10},{10,11},{12,13},{... | collective-permute-start | bytes 294920 | tf_op jit(solution)/shard_map/while/body/eval_jaxpr/ppermute | solution.py:19
  306.9 6.3 %collective-permute-start.1 = (bf16[3,16,768]{2,1,0:T(8,128)(2,1)S(1)}, bf16[3,16,768]{2,1,0:T(8,128)(2,1)S(1)}, u32[]{:S(2)}, u32[]{:S(2)}) collective-permute-start(bf16[3,16,768]{2,1,0:T(8,128)(2,1)S(1)} %get-tuple-element.1228), channel_id=1, source_target_pairs={{4,0},{8,4},{12,8},{5,1},{9,5},{13,9},{6,2},{10,6},{14,10},{7,3},{... | collective-permute-start | bytes 221192 | tf_op jit(solution)/shard_map/while/body/eval_jaxpr/ppermute | solution.py:30
  308.2 6.6 %collective-permute-start.2 = (bf16[3,16,768]{2,1,0:T(8,128)(2,1)S(1)}, bf16[3,16,768]{2,1,0:T(8,128)(2,1)S(1)}, u32[]{:S(2)}, u32[]{:S(2)}) collective-permute-start(bf16[3,16,768]{2,1,0:T(8,128)(2,1)S(1)} %get-tuple-element.1229), channel_id=1, source_target_pairs={{0,4},{4,8},{8,12},{1,5},{5,9},{9,13},{2,6},{6,10},{10,14},{3,7},{... | collective-permute-start | bytes 221192 | tf_op jit(solution)/shard_map/while/body/eval_jaxpr/ppermute | solution.py:27
  315.5 24.8 %collective-permute-start.3 = (bf16[4,16,768]{2,1,0:T(8,128)(2,1)S(1)}, bf16[4,16,768]{2,1,0:T(8,128)(2,1)S(1)}, u32[]{:S(2)}, u32[]{:S(2)}) collective-permute-start(bf16[4,16,768]{2,1,0:T(8,128)(2,1)S(1)} %broadcast_select_fusion.4), channel_id=1, source_target_pairs={{1,0},{2,1},{3,2},{5,4},{6,5},{7,6},{9,8},{10,9},{11,10},{13,12},{... | collective-permute-start | bytes 294920 | tf_op jit(solution)/shard_map/while/body/eval_jaxpr/ppermute | solution.py:19
  341.4 7.1 %collective-permute-start.4 = (bf16[3,16,768]{2,1,0:T(8,128)(2,1)S(1)}, bf16[3,16,768]{2,1,0:T(8,128)(2,1)S(1)}, u32[]{:S(2)}, u32[]{:S(2)}) collective-permute-start(bf16[3,16,768]{2,1,0:T(8,128)(2,1)S(1)} %get-tuple-element.1258), channel_id=1, source_target_pairs={{4,0},{8,4},{12,8},{5,1},{9,5},{13,9},{6,2},{10,6},{14,10},{7,3},{... | collective-permute-start | bytes 221192 | tf_op jit(solution)/shard_map/while/body/eval_jaxpr/ppermute | solution.py:30
  342.7 6.6 %collective-permute-start.5 = (bf16[3,16,768]{2,1,0:T(8,128)(2,1)S(1)}, bf16[3,16,768]{2,1,0:T(8,128)(2,1)S(1)}, u32[]{:S(2)}, u32[]{:S(2)}) collective-permute-start(bf16[3,16,768]{2,1,0:T(8,128)(2,1)S(1)} %get-tuple-element.1259), channel_id=1, source_target_pairs={{0,4},{4,8},{8,12},{1,5},{5,9},{9,13},{2,6},{6,10},{10,14},{3,7},{... | collective-permute-start | bytes 221192 | tf_op jit(solution)/shard_map/while/body/eval_jaxpr/ppermute | solution.py:27
  350.6 6.8 %collective-permute-start.3 = (bf16[4,16,768]{2,1,0:T(8,128)(2,1)S(1)}, bf16[4,16,768]{2,1,0:T(8,128)(2,1)S(1)}, u32[]{:S(2)}, u32[]{:S(2)}) collective-permute-start(bf16[4,16,768]{2,1,0:T(8,128)(2,1)S(1)} %broadcast_select_fusion.4), channel_id=1, source_target_pairs={{1,0},{2,1},{3,2},{5,4},{6,5},{7,6},{9,8},{10,9},{11,10},{13,12},{... | collective-permute-start | bytes 294920 | tf_op jit(solution)/shard_map/while/body/eval_jaxpr/ppermute | solution.py:19
  358.5 7.1 %collective-permute-start.4 = (bf16[3,16,768]{2,1,0:T(8,128)(2,1)S(1)}, bf16[3,16,768]{2,1,0:T(8,128)(2,1)S(1)}, u32[]{:S(2)}, u32[]{:S(2)}) collective-permute-start(bf16[3,16,768]{2,1,0:T(8,128)(2,1)S(1)} %get-tuple-element.1258), channel_id=1, source_target_pairs={{4,0},{8,4},{12,8},{5,1},{9,5},{13,9},{6,2},{10,6},{14,10},{7,3},{... | collective-permute-start | bytes 221192 | tf_op jit(solution)/shard_map/while/body/eval_jaxpr/ppermute | solution.py:30
  359.8 6.6 %collective-permute-start.5 = (bf16[3,16,768]{2,1,0:T(8,128)(2,1)S(1)}, bf16[3,16,768]{2,1,0:T(8,128)(2,1)S(1)}, u32[]{:S(2)}, u32[]{:S(2)}) collective-permute-start(bf16[3,16,768]{2,1,0:T(8,128)(2,1)S(1)} %get-tuple-element.1259), channel_id=1, source_target_pairs={{0,4},{4,8},{8,12},{1,5},{5,9},{9,13},{2,6},{6,10},{10,14},{3,7},{... | collective-permute-start | bytes 221192 | tf_op jit(solution)/shard_map/while/body/eval_jaxpr/ppermute | solution.py:27
  367.7 17.8 %collective-permute-start.3 = (bf16[4,16,768]{2,1,0:T(8,128)(2,1)S(1)}, bf16[4,16,768]{2,1,0:T(8,128)(2,1)S(1)}, u32[]{:S(2)}, u32[]{:S(2)}) collective-permute-start(bf16[4,16,768]{2,1,0:T(8,128)(2,1)S(1)} %broadcast_select_fusion.4), channel_id=1, source_target_pairs={{1,0},{2,1},{3,2},{5,4},{6,5},{7,6},{9,8},{10,9},{11,10},{13,12},{... | collective-permute-start | bytes 294920 | tf_op jit(solution)/shard_map/while/body/eval_jaxpr/ppermute | solution.py:19
  386.6 7.1 %collective-permute-start.4 = (bf16[3,16,768]{2,1,0:T(8,128)(2,1)S(1)}, bf16[3,16,768]{2,1,0:T(8,128)(2,1)S(1)}, u32[]{:S(2)}, u32[]{:S(2)}) collective-permute-start(bf16[3,16,768]{2,1,0:T(8,128)(2,1)S(1)} %get-tuple-element.1258), channel_id=1, source_target_pairs={{4,0},{8,4},{12,8},{5,1},{9,5},{13,9},{6,2},{10,6},{14,10},{7,3},{... | collective-permute-start | bytes 221192 | tf_op jit(solution)/shard_map/while/body/eval_jaxpr/ppermute | solution.py:30
  387.9 6.6 %collective-permute-start.5 = (bf16[3,16,768]{2,1,0:T(8,128)(2,1)S(1)}, bf16[3,16,768]{2,1,0:T(8,128)(2,1)S(1)}, u32[]{:S(2)}, u32[]{:S(2)}) collective-permute-start(bf16[3,16,768]{2,1,0:T(8,128)(2,1)S(1)} %get-tuple-element.1259), channel_id=1, source_target_pairs={{0,4},{4,8},{8,12},{1,5},{5,9},{9,13},{2,6},{6,10},{10,14},{3,7},{... | collective-permute-start | bytes 221192 | tf_op jit(solution)/shard_map/while/body/eval_jaxpr/ppermute | solution.py:27
  395.9 39.4 %collective-permute-start.3 = (bf16[4,16,768]{2,1,0:T(8,128)(2,1)S(1)}, bf16[4,16,768]{2,1,0:T(8,128)(2,1)S(1)}, u32[]{:S(2)}, u32[]{:S(2)}) collective-permute-start(bf16[4,16,768]{2,1,0:T(8,128)(2,1)S(1)} %broadcast_select_fusion.4), channel_id=1, source_target_pairs={{1,0},{2,1},{3,2},{5,4},{6,5},{7,6},{9,8},{10,9},{11,10},{13,12},{... | collective-permute-start | bytes 294920 | tf_op jit(solution)/shard_map/while/body/eval_jaxpr/ppermute | solution.py:19
  447.9 7.1 %collective-permute-start.4 = (bf16[3,16,768]{2,1,0:T(8,128)(2,1)S(1)}, bf16[3,16,768]{2,1,0:T(8,128)(2,1)S(1)}, u32[]{:S(2)}, u32[]{:S(2)}) collective-permute-start(bf16[3,16,768]{2,1,0:T(8,128)(2,1)S(1)} %get-tuple-element.1258), channel_id=1, source_target_pairs={{4,0},{8,4},{12,8},{5,1},{9,5},{13,9},{6,2},{10,6},{14,10},{7,3},{... | collective-permute-start | bytes 221192 | tf_op jit(solution)/shard_map/while/body/eval_jaxpr/ppermute | solution.py:30
  449.2 6.6 %collective-permute-start.5 = (bf16[3,16,768]{2,1,0:T(8,128)(2,1)S(1)}, bf16[3,16,768]{2,1,0:T(8,128)(2,1)S(1)}, u32[]{:S(2)}, u32[]{:S(2)}) collective-permute-start(bf16[3,16,768]{2,1,0:T(8,128)(2,1)S(1)} %get-tuple-element.1259), channel_id=1, source_target_pairs={{0,4},{4,8},{8,12},{1,5},{5,9},{9,13},{2,6},{6,10},{10,14},{3,7},{... | collective-permute-start | bytes 221192 | tf_op jit(solution)/shard_map/while/body/eval_jaxpr/ppermute | solution.py:27
  457.1 6.6 %collective-permute-start.3 = (bf16[4,16,768]{2,1,0:T(8,128)(2,1)S(1)}, bf16[4,16,768]{2,1,0:T(8,128)(2,1)S(1)}, u32[]{:S(2)}, u32[]{:S(2)}) collective-permute-start(bf16[4,16,768]{2,1,0:T(8,128)(2,1)S(1)} %broadcast_select_fusion.4), channel_id=1, source_target_pairs={{1,0},{2,1},{3,2},{5,4},{6,5},{7,6},{9,8},{10,9},{11,10},{13,12},{... | collective-permute-start | bytes 294920 | tf_op jit(solution)/shard_map/while/body/eval_jaxpr/ppermute | solution.py:19
  476.3 7.1 %collective-permute-start.4 = (bf16[3,16,768]{2,1,0:T(8,128)(2,1)S(1)}, bf16[3,16,768]{2,1,0:T(8,128)(2,1)S(1)}, u32[]{:S(2)}, u32[]{:S(2)}) collective-permute-start(bf16[3,16,768]{2,1,0:T(8,128)(2,1)S(1)} %get-tuple-element.1258), channel_id=1, source_target_pairs={{4,0},{8,4},{12,8},{5,1},{9,5},{13,9},{6,2},{10,6},{14,10},{7,3},{... | collective-permute-start | bytes 221192 | tf_op jit(solution)/shard_map/while/body/eval_jaxpr/ppermute | solution.py:30
  477.6 6.6 %collective-permute-start.5 = (bf16[3,16,768]{2,1,0:T(8,128)(2,1)S(1)}, bf16[3,16,768]{2,1,0:T(8,128)(2,1)S(1)}, u32[]{:S(2)}, u32[]{:S(2)}) collective-permute-start(bf16[3,16,768]{2,1,0:T(8,128)(2,1)S(1)} %get-tuple-element.1259), channel_id=1, source_target_pairs={{0,4},{4,8},{8,12},{1,5},{5,9},{9,13},{2,6},{6,10},{10,14},{3,7},{... | collective-permute-start | bytes 221192 | tf_op jit(solution)/shard_map/while/body/eval_jaxpr/ppermute | solution.py:27
  485.6 6.7 %collective-permute-start.3 = (bf16[4,16,768]{2,1,0:T(8,128)(2,1)S(1)}, bf16[4,16,768]{2,1,0:T(8,128)(2,1)S(1)}, u32[]{:S(2)}, u32[]{:S(2)}) collective-permute-start(bf16[4,16,768]{2,1,0:T(8,128)(2,1)S(1)} %broadcast_select_fusion.4), channel_id=1, source_target_pairs={{1,0},{2,1},{3,2},{5,4},{6,5},{7,6},{9,8},{10,9},{11,10},{13,12},{... | collective-permute-start | bytes 294920 | tf_op jit(solution)/shard_map/while/body/eval_jaxpr/ppermute | solution.py:19
  505.0 7.1 %collective-permute-start.4 = (bf16[3,16,768]{2,1,0:T(8,128)(2,1)S(1)}, bf16[3,16,768]{2,1,0:T(8,128)(2,1)S(1)}, u32[]{:S(2)}, u32[]{:S(2)}) collective-permute-start(bf16[3,16,768]{2,1,0:T(8,128)(2,1)S(1)} %get-tuple-element.1258), channel_id=1, source_target_pairs={{4,0},{8,4},{12,8},{5,1},{9,5},{13,9},{6,2},{10,6},{14,10},{7,3},{... | collective-permute-start | bytes 221192 | tf_op jit(solution)/shard_map/while/body/eval_jaxpr/ppermute | solution.py:30
  506.3 6.6 %collective-permute-start.5 = (bf16[3,16,768]{2,1,0:T(8,128)(2,1)S(1)}, bf16[3,16,768]{2,1,0:T(8,128)(2,1)S(1)}, u32[]{:S(2)}, u32[]{:S(2)}) collective-permute-start(bf16[3,16,768]{2,1,0:T(8,128)(2,1)S(1)} %get-tuple-element.1259), channel_id=1, source_target_pairs={{0,4},{4,8},{8,12},{1,5},{5,9},{9,13},{2,6},{6,10},{10,14},{3,7},{... | collective-permute-start | bytes 221192 | tf_op jit(solution)/shard_map/while/body/eval_jaxpr/ppermute | solution.py:27
  514.2 6.4 %collective-permute-start.3 = (bf16[4,16,768]{2,1,0:T(8,128)(2,1)S(1)}, bf16[4,16,768]{2,1,0:T(8,128)(2,1)S(1)}, u32[]{:S(2)}, u32[]{:S(2)}) collective-permute-start(bf16[4,16,768]{2,1,0:T(8,128)(2,1)S(1)} %broadcast_select_fusion.4), channel_id=1, source_target_pairs={{1,0},{2,1},{3,2},{5,4},{6,5},{7,6},{9,8},{10,9},{11,10},{13,12},{... | collective-permute-start | bytes 294920 | tf_op jit(solution)/shard_map/while/body/eval_jaxpr/ppermute | solution.py:19
  533.3 7.1 %collective-permute-start.4 = (bf16[3,16,768]{2,1,0:T(8,128)(2,1)S(1)}, bf16[3,16,768]{2,1,0:T(8,128)(2,1)S(1)}, u32[]{:S(2)}, u32[]{:S(2)}) collective-permute-start(bf16[3,16,768]{2,1,0:T(8,128)(2,1)S(1)} %get-tuple-element.1258), channel_id=1, source_target_pairs={{4,0},{8,4},{12,8},{5,1},{9,5},{13,9},{6,2},{10,6},{14,10},{7,3},{... | collective-permute-start | bytes 221192 | tf_op jit(solution)/shard_map/while/body/eval_jaxpr/ppermute | solution.py:30
  534.6 6.6 %collective-permute-start.5 = (bf16[3,16,768]{2,1,0:T(8,128)(2,1)S(1)}, bf16[3,16,768]{2,1,0:T(8,128)(2,1)S(1)}, u32[]{:S(2)}, u32[]{:S(2)}) collective-permute-start(bf16[3,16,768]{2,1,0:T(8,128)(2,1)S(1)} %get-tuple-element.1259), channel_id=1, source_target_pairs={{0,4},{4,8},{8,12},{1,5},{5,9},{9,13},{2,6},{6,10},{10,14},{3,7},{... | collective-permute-start | bytes 221192 | tf_op jit(solution)/shard_map/while/body/eval_jaxpr/ppermute | solution.py:27
Sparse Core Ops, SparseCore 0:
  9.6 53.1 all-gather.4
  64.4 49.2 all-gather.6
  543.4 36.2 all-reduce.5
where the time goes:
time: 595 us; the launch traced here: 588 us
  waiting for transfers between devices  209 us (35%)
  starting transfers between devices  130 us (22%)
  local copies, waits for them, and re-layouts  86.1 us (14%)
  other arithmetic  81.1 us (14%)
  matrix products  33.8 us (6%)
  blocking collectives  21.2 us (4%)
  between operations  13.8 us (2%)
  loops' own time  12.3 us (2%)
    ppermute x14, waiting for transfers between devices, shifted(): lax.ppermute(value, axis, [(source, source + steps) for source in range(f...  70.1 us
    ppermute x14, starting transfers between devices, with_halo(): lax.ppermute(lax.slice_in_dim(block, block.shape[dim] - width, None, axis...  65.5 us
    all_gather x1, waiting for transfers between devices, per_device(): lax.all_gather(expand_weight[0], 'rows', axis=0, tiled=True)  52.5 us
    all_gather x1, waiting for transfers between devices, per_device(): lax.all_gather(reduce_weight[0], 'rows', axis=0, tiled=True)  50.9 us
    ppermute x14, starting transfers between devices, shifted(): lax.ppermute(value, axis, [(source, source + steps) for source in range(f...  46.5 us
    slice x21, local copies, waits for them, and re-layouts, depthwise_back(): kernel[row_off * KS + col_off]  28.6 us
    slice x12, local copies, waits for them, and re-layouts, depthwise(): kernel[row_off * KS + col_off]  23.8 us
    psum x1, blocking collectives, per_device(): lax.psum((totals[0], totals[1], totals[2], totals[3], totals[4]), 'rows')  21.2 us
  transfers between devices with their start and end apart: 45, of which 31 were waited for; matrix products, arithmetic and copies ran while one was open for 7% of the time, Pallas kernels for 0%

commit v1 on v0

v1 whole, which is shorter than its diff:
```python
import functools
import math

import jax
import jax.numpy as jnp
from jax import lax
from jax.experimental import pallas as pl
from jax.experimental.pallas import tpu as pltpu
from jax.sharding import PartitionSpec as P

KS = 7
MARGIN = KS // 2
LANES = 128
SIDE = 8
EPSILON = 1e-06
SQRT_HALF = 0.7071067811865476
INV_ROOT_TAU = 0.3989422804014327
MESH = pl.DeviceIdType.MESH


def contract_last(left, right):
    return lax.dot_general(
        left, right, (((1,), (1,)), ((), ())), preferred_element_type=jnp.float32
    )


def eight_rows(value):
    tokens, channels = value.shape
    return value.reshape(tokens // 8, 8, channels).sum(axis=0)


def chain_kernel(
    sections, slabs, loss_scale,
    latent, target, w_expand, b_expand, w_reduce, b_reduce, taps, offset, gain, shift, scale,
    kernel_out, offset_out, gain_out, shift_out, scale_out,
    frame, output, normed_s, inverse_s, bend_s, branch_s,
    cot_in, slope_frame, cot, slope_low, slope_s, grid_s, token_s, pad, taps_next,
    kernel_sum, small_sum, slots,
    fwd_send, edge_send, fwd_recv, bwd_send, bwd_recv, tap_send, tap_recv, sum_send, sum_recv,
):
    sec = lax.axis_index("section")
    row = lax.axis_index("rows")
    micro, height, breadth, channels = latent.shape
    tokens = height * breadth
    hidden_units = w_expand.shape[1]
    piece = 512 if hidden_units % 512 == 0 else LANES
    tall = height + 2 * MARGIN
    first, last = sec == 0, sec == sections - 1
    has_low, has_high = row > 0, row < slabs - 1

    barrier = pltpu.get_barrier_semaphore()
    greeted = jnp.int32(slabs - 1)
    for other in range(slabs):
        @pl.when(row != other)
        def _(other=other):
            pl.semaphore_signal(
                barrier, inc=1, device_id={"section": sec, "rows": other}, device_id_type=MESH
            )
    for ds in (-1, 1):
        for dr in (-1, 0, 1):
            there = (sec + ds >= 0) & (sec + ds < sections) & (row + dr >= 0) & (row + dr < slabs)

            @pl.when(there)
            def _(ds=ds, dr=dr):
                pl.semaphore_signal(
                    barrier, inc=1,
                    device_id={"section": sec + ds, "rows": row + dr}, device_id_type=MESH,
                )
            greeted = greeted + jnp.where(there, 1, 0)
    pl.semaphore_wait(barrier, greeted)

    def remote(source, dest, send, recv, to_sec, to_row):
        return pltpu.make_async_remote_copy(
            src_ref=source, dst_ref=dest, send_sem=send, recv_sem=recv,
            device_id={"section": to_sec, "rows": to_row}, device_id_type=MESH,
        )

    def grid_copies(source, dest, m, send, recv, to_sec):
        low, high = jnp.maximum(row - 1, 0), jnp.minimum(row + 1, slabs - 1)
        return (
            remote(source.at[m], dest.at[m, pl.ds(MARGIN, height)],
                   send.at[m, 0], recv.at[m, 0], to_sec, row),
            remote(source.at[m, pl.ds(height - MARGIN, MARGIN)], dest.at[m, pl.ds(0, MARGIN)],
                   send.at[m, 1], recv.at[m, 1], to_sec, high),
            remote(source.at[m, pl.ds(0, MARGIN)], dest.at[m, pl.ds(MARGIN + height, MARGIN)],
                   send.at[m, 2], recv.at[m, 2], to_sec, low),
        )

    def fwd_copies(m):
        return grid_copies(output, frame, m, fwd_send, fwd_recv, next_sec)

    def edge_copies(m):
        return grid_copies(latent, frame, m, edge_send, fwd_recv, sec)

    next_sec = jnp.minimum(sec + 1, sections - 1)
    prev_sec = jnp.maximum(sec - 1, 0)
    tap_copy = remote(taps, taps_next, tap_send, tap_recv, prev_sec, row)

    @pl.when(sec > 0)
    def _():
        tap_copy.start()

    @pl.when(first)
    def _():
        for m in range(micro):
            _, down, up = edge_copies(m)

            @pl.when(has_high)
            def _():
                down.start()

            @pl.when(has_low)
            def _():
                up.start()
            frame[m, pl.ds(MARGIN, height)] = latent[m]

    edge = jnp.zeros((micro, MARGIN, breadth, channels), jnp.bfloat16)

    @pl.when(row == 0)
    def _():
        frame[:, pl.ds(0, MARGIN)] = edge
        slope_frame[:, pl.ds(0, MARGIN)] = edge

    @pl.when(row == slabs - 1)
    def _():
        frame[:, pl.ds(MARGIN + height, MARGIN)] = edge
        slope_frame[:, pl.ds(MARGIN + height, MARGIN)] = edge

    pad[:, pl.ds(0, SIDE)] = jnp.zeros((tall, SIDE, channels), jnp.float32)
    pad[:, pl.ds(SIDE + breadth, SIDE)] = jnp.zeros((tall, SIDE, channels), jnp.float32)
    kernel_sum[...] = jnp.zeros_like(kernel_sum)
    small_sum[...] = jnp.zeros_like(small_sum)

    def lanes_of(c):
        return pl.ds(pl.multiple_of(c * LANES, LANES), LANES)

    def columns(col_off, lanes):
        return pad[:, pl.ds(SIDE - MARGIN + col_off, breadth), lanes]

    @pl.loop(0, micro)
    def _(m):
        mid, down, up = fwd_copies(m)

        @pl.when(sec > 0)
        def _():
            mid.wait_recv()

        @pl.when(has_low)
        def _():
            down.wait_recv()

        @pl.when(has_high)
        def _():
            up.wait_recv()

        pad[:, pl.ds(SIDE, breadth)] = frame[m].astype(jnp.float32)

        @pl.loop(0, channels // LANES)
        def _(c):
            lanes = lanes_of(c)
            summed = jnp.zeros((height, breadth, LANES), jnp.float32) + offset[:, lanes]
            for b in range(KS):
                column = columns(b, lanes)
                for a in range(KS):
                    summed = summed + taps[pl.ds(KS * a + b, 1), lanes] * column[a : a + height]
            grid_s[:, :, lanes] = summed

        mixed = grid_s[...].reshape(tokens, channels)
        centred = mixed - jnp.mean(mixed, axis=-1, keepdims=True)
        variance = jnp.mean(centred * centred, axis=-1, keepdims=True)
        inverse = lax.rsqrt(variance + EPSILON)
        normed = centred * inverse
        normed_s[m] = normed
        inverse_s[m] = jnp.broadcast_to(inverse, (tokens, LANES))
        inputs = (normed * gain[...] + shift[...]).astype(jnp.bfloat16)
        branch = jnp.zeros((tokens, channels), jnp.float32) + b_reduce[...]
        for f in range(hidden_units // piece):
            units = pl.ds(f * piece, piece)
            hidden = (
                jnp.dot(inputs, w_expand[:, units], preferred_element_type=jnp.float32)
                + b_expand[:, units]
            )
            below = 0.5 * (1.0 + lax.erf(hidden * SQRT_HALF))
            bend_s[m, :, units] = below + hidden * jnp.exp(-0.5 * hidden * hidden) * INV_ROOT_TAU
            active = (hidden * below).astype(jnp.bfloat16)
            branch = branch + jnp.dot(active, w_reduce[units, :], preferred_element_type=jnp.float32)
        branch_s[m] = branch
        source = frame[m, pl.ds(MARGIN, height)].astype(jnp.float32)
        grown = source + (scale[...] * branch).reshape(height, breadth, channels)
        output[m] = grown.astype(jnp.bfloat16)

        @pl.when(sec < sections - 1)
        def _():
            mid.start()

            @pl.when(has_high)
            def _():
                down.start()

            @pl.when(has_low)
            def _():
                up.start()

    @pl.when(sec < sections - 1)
    def _():
        tap_copy.wait_recv()

    def bwd_copies(m):
        return grid_copies(slope_low, slope_frame, m, bwd_send, bwd_recv, prev_sec) + (
            remote(cot.at[m], cot_in.at[m], bwd_send.at[m, 3], bwd_recv.at[m, 3], prev_sec, row),
        )

    @pl.loop(0, micro)
    def _(m):
        mid, down, up, whole = bwd_copies(m)

        @pl.when(last)
        def _():
            gap = output[m].astype(jnp.float32) - target[m].astype(jnp.float32)
            cot[m] = (gap * loss_scale).astype(jnp.bfloat16)

        @pl.when(sec < sections - 1)
        def _():
            mid.wait_recv()
            whole.wait_recv()

            @pl.when(has_low)
            def _():
                down.wait_recv()

            @pl.when(has_high)
            def _():
                up.wait_recv()

            pad[:, pl.ds(SIDE, breadth)] = slope_frame[m].astype(jnp.float32)

            @pl.loop(0, channels // LANES)
            def _(c):
                lanes = lanes_of(c)
                summed = jnp.zeros((height, breadth, LANES), jnp.float32)
                for b in range(KS):
                    column = columns(2 * MARGIN - b, lanes)
                    for a in range(KS):
                        begin = 2 * MARGIN - a
                        summed = (
                            summed
                            + taps_next[pl.ds(KS * a + b, 1), lanes] * column[begin : begin + height]
                        )
                passed = cot_in[m, :, :, lanes].astype(jnp.float32) + summed
                cot[m, :, :, lanes] = passed.astype(jnp.bfloat16)

        arrived = cot[m].astype(jnp.float32).reshape(tokens, channels)
        small_sum[3] += eight_rows(arrived * branch_s[m])
        reduced = (arrived * scale[...]).astype(jnp.bfloat16)
        normal_slope = jnp.zeros((tokens, channels), jnp.float32)
        for f in range(hidden_units // piece):
            units = pl.ds(f * piece, piece)
            spread = contract_last(reduced, w_reduce[units, :])
            hidden_slope = (spread * bend_s[m, :, units]).astype(jnp.bfloat16)
            normal_slope = normal_slope + contract_last(hidden_slope, w_expand[:, units])
        normed = normed_s[m]
        scaled = normal_slope * gain[...]
        token_s[...] = normal_slope
        slope = (
            scaled
            - jnp.mean(scaled, axis=-1, keepdims=True)
            - normed * jnp.mean(scaled * normed, axis=-1, keepdims=True)
        ) * inverse_s[m][:, :1]
        slope_s[...] = slope.reshape(height, breadth, channels)

        @pl.when(sec > 0)
        def _():
            slope_low[m] = slope_s[...].astype(jnp.bfloat16)
            mid.start()
            whole.start()

            @pl.when(has_high)
            def _():
                down.start()

            @pl.when(has_low)
            def _():
                up.start()

        small_sum[0] += eight_rows(slope_s[...].reshape(tokens, channels))
        small_sum[1] += eight_rows(token_s[...] * normed_s[m])
        small_sum[2] += eight_rows(token_s[...])
        pad[:, pl.ds(SIDE, breadth)] = frame[m].astype(jnp.float32)

        @pl.loop(0, channels // LANES)
        def _(c):
            lanes = lanes_of(c)
            own = slope_s[:, :, lanes]
            for b in range(KS):
                column = columns(b, lanes)
                for a in range(KS):
                    term = (own * column[a : a + height]).reshape(tokens, LANES)
                    kernel_sum[KS * a + b, :, lanes] += eight_rows(term)

    spots = KS * KS
    slots[row, pl.ds(0, spots)] = jnp.sum(kernel_sum[...], axis=1)
    slots[row, pl.ds(spots, 4)] = jnp.sum(small_sum[...], axis=1)

    def sum_copy(other, send_at, recv_at):
        return remote(slots.at[row], slots.at[row], sum_send.at[send_at], sum_recv.at[recv_at],
                      sec, other)

    for other in range(slabs):
        @pl.when(row != other)
        def _(other=other):
            sum_copy(other, other, row).start()
    for other in range(slabs):
        @pl.when(row != other)
        def _(other=other):
            copy = remote(slots.at[other], slots.at[other], sum_send.at[other],
                          sum_recv.at[other], sec, other)
            copy.wait_recv()
    total = slots[0]
    for other in range(1, slabs):
        total = total + slots[other]
    kernel_out[...] = total[:spots]
    offset_out[...] = total[spots : spots + 1]
    gain_out[...] = total[spots + 1 : spots + 2]
    shift_out[...] = total[spots + 2 : spots + 3]
    scale_out[...] = total[spots + 3 : spots + 4]

    for other in range(slabs):
        @pl.when(row != other)
        def _(other=other):
            sum_copy(other, other, row).wait_send()

    @pl.when(sec > 0)
    def _():
        tap_copy.wait_send()

    @pl.loop(0, micro)
    def _(m):
        mid, down, up = fwd_copies(m)

        @pl.when(sec < sections - 1)
        def _():
            mid.wait_send()

            @pl.when(has_high)
            def _():
                down.wait_send()

            @pl.when(has_low)
            def _():
                up.wait_send()

        @pl.when(first)
        def _():
            _, edge_down, edge_up = edge_copies(m)

            @pl.when(has_high)
            def _():
                edge_down.wait_send()

            @pl.when(has_low)
            def _():
                edge_up.wait_send()

        mid, down, up, whole = bwd_copies(m)

        @pl.when(sec > 0)
        def _():
            mid.wait_send()
            whole.wait_send()

            @pl.when(has_high)
            def _():
                down.wait_send()

            @pl.when(has_low)
            def _():
                up.wait_send()


def per_device(
    latent, target, expand_weight, expand_bias, reduce_weight, reduce_bias,
    depth_kernel, depth_offset, norm_gain, norm_shift, layer_scale,
):
    sections, slabs = lax.axis_size("section"), lax.axis_size("rows")
    micro, height, breadth, channels = latent.shape
    hidden_units = expand_weight.shape[2]
    tokens = height * breadth
    tall = height + 2 * MARGIN
    spots = KS * KS
    loss_scale = 1.0 / math.sqrt(micro * height * slabs * breadth)
    w_expand = lax.all_gather(expand_weight[0], "rows", axis=0, tiled=True)
    w_reduce = lax.all_gather(reduce_weight[0], "rows", axis=0, tiled=True)
    low, wide = jnp.bfloat16, jnp.float32
    dma, vmem = pltpu.SemaphoreType.DMA, pltpu.VMEM
    found = pl.pallas_call(
        functools.partial(chain_kernel, sections, slabs, loss_scale),
        out_shape=(jax.ShapeDtypeStruct((spots, channels), wide),)
        + (jax.ShapeDtypeStruct((1, channels), wide),) * 4,
        in_specs=[pl.BlockSpec(memory_space=vmem)] * 11,
        out_specs=(pl.BlockSpec(memory_space=vmem),) * 5,
        scratch_shapes=[
            vmem((micro, tall, breadth, channels), low),
            vmem((micro, height, breadth, channels), low),
            vmem((micro, tokens, channels), wide),
            vmem((micro, tokens, LANES), wide),
            vmem((micro, tokens, hidden_units), wide),
            vmem((micro, tokens, channels), wide),
            vmem((micro, height, breadth, channels), low),
            vmem((micro, tall, breadth, channels), low),
            vmem((micro, height, breadth, channels), low),
            vmem((micro, height, breadth, channels), low),
            vmem((height, breadth, channels), wide),
            vmem((height, breadth, channels), wide),
            vmem((tokens, channels), wide),
            vmem((tall, breadth + 2 * SIDE, channels), wide),
            vmem((spots, channels), wide),
            vmem((spots, 8, channels), wide),
            vmem((4, 8, channels), wide),
            vmem((slabs, spots + 4, channels), wide),
            dma((micro, 3)), dma((micro, 3)), dma((micro, 3)),
            dma((micro, 4)), dma((micro, 4)),
            dma, dma,
            dma((slabs,)), dma((slabs,)),
        ],
        compiler_params=pltpu.CompilerParams(
            collective_id=0, has_side_effects=True, vmem_limit_bytes=48 * 1024 * 1024
        ),
        name="block_chain",
    )(
        latent, target, w_expand, expand_bias, w_reduce, reduce_bias,
        depth_kernel[0], depth_offset, norm_gain, norm_shift, layer_scale,
    )
    return (found[0][None],) + tuple(found[1:])


def solution(mesh):
    image = P("groups", "rows", None, None)
    matrix, vector = P("section", "rows", None), P("section", None)
    both = ("groups", "section")
    return jax.shard_map(
        per_device,
        mesh=mesh,
        in_specs=(
            image, image, matrix, vector, matrix, vector,
            P("section", None, None), vector, vector, vector, vector,
        ),
        out_specs=(P(both, None, None),) + (P(both, None),) * 4,
        check_vma=False,
    )
```

time: 595 us -> 224 us (0.38)
  starting transfers between devices: 130 us -> 0.08 us
  waiting for transfers between devices: 209 us -> 105 us
  Pallas kernels: 0 us -> 88.2 us
  other arithmetic: 81.1 us -> 0 us
  local copies, waits for them, and re-layouts: 86.1 us -> 13.5 us
  matrix products: 33.8 us -> 0 us
  blocking collectives: 21.2 us -> 0 us
  loops' own time: 12.3 us -> 0 us
    ppermute x42 -> x0, starting transfers between devices: 130 us -> none  [the longest x14 65.5 us: with_halo(): lax.ppermute(lax.slice_in_dim(block, block.shape[dim] - width, None, axis...]
    ppermute x42 -> x0, waiting for transfers between devices: 89.4 us -> none  [the longest x14 70.1 us: shifted(): lax.ppermute(value, axis, [(source, source + steps) for source in range(f...]
    pallas_call x0 -> x1, Pallas kernels: none -> 88.2 us  [per_device(): pl.pallas_call(functools.partial(chain_kernel, sections, slabs, loss_scal...]
    slice x47 -> x0, local copies, waits for them, and re-layouts: 52.5 us -> none  [the longest x21 28.6 us: depthwise_back(): kernel[row_off * KS + col_off]]
    dot_general x12 -> x0, matrix products: 33.8 us -> none  [the longest x4 14.5 us: project_forward(): jnp.dot(active, w_reduce, preferred_element_type=jnp.float32) + b_reduce]
    reduce_sum x32 -> x0, other arithmetic: 27.3 us -> none  [the longest x8 12.6 us: normalize(): centre = jnp.mean(flat, axis=-1, keepdims=True)]
    select_n x21 -> x0, other arithmetic: 21.8 us -> none  [the longest x7 8.58 us: backward_moment(): passed = jnp.where(valid, passed, spare_grid)]
    psum x1 -> x0, blocking collectives: 21.2 us -> none  [per_device(): lax.psum((totals[0], totals[1], totals[2], totals[3], totals[4]), 'rows')]
  transfers between devices with their start and end apart: 45 -> 2, of which waited for: 31 -> 2; matrix products, arithmetic and copies ran while one was open for 7% -> 0% of each run, Pallas kernels for 0% -> 0%
where the time goes in v1:
time: 224 us; the launch traced here: 221 us
  waiting for transfers between devices  105 us (47%)
  Pallas kernels  88.2 us (39%)
  between operations  14.1 us (6%)
  local copies, waits for them, and re-layouts  13.5 us (6%)
    pallas_call x1, Pallas kernels, per_device(): pl.pallas_call(functools.partial(chain_kernel, sections, slabs, loss_scal...  88.2 us
    all_gather x1, waiting for transfers between devices, per_device(): w_expand = lax.all_gather(expand_weight[0], 'rows', axis=0, tiled=True)  53.2 us
    all_gather x1, waiting for transfers between devices, per_device(): w_reduce = lax.all_gather(reduce_weight[0], 'rows', axis=0, tiled=True)  50.9 us
    unnamed x26, local copies, waits for them, and re-layouts  13.5 us
  transfers between devices with their start and end apart: 2, of which 2 were waited for; matrix products, arithmetic and copies ran while one was open for 0% of the time, Pallas kernels for 0%

profile of v1, /device:TPU:0, one launch (start us, length us, event | category | flops | bytes accessed | tf_op | source)
XLA Modules:
  0.0 221.3 jit_solution(11016095619495502120)
XLA Ops:
  7.2 0.0 all-gather.5.cloned.1.call-start
  7.2 0.7 all-gather.5.cloned.1.call-update
  7.9 0.0 all-gather.7.cloned.1.call-start
  7.9 0.7 all-gather.7.cloned.1.call-update
  8.6 0.9 copy.19
  9.6 53.2 %all-gather.5.cloned.1.call-done = bf16[1,768,1536]{2,1,0:T(8,128)(2,1)} async-done(((bf16[1,192,1536]{2,1,0:T(8,128)(2,1)}), bf16[1,768,1536]{2,1,0:T(8,128)(2,1)}) %all-gather.5.cloned.1.call-update) | async-done | bytes 2359312 | tf_op jit(solution)/shard_map/all_gather | solution.py:391
  62.8 50.9 %all-gather.7.cloned.1.call-done = bf16[1,1536,768]{2,1,0:T(8,128)(2,1)} async-done(((bf16[1,384,768]{2,1,0:T(8,128)(2,1)}), bf16[1,1536,768]{2,1,0:T(8,128)(2,1)}) %all-gather.7.cloned.1.call-update) | async-done | bytes 2359312 | tf_op jit(solution)/shard_map/all_gather | solution.py:392
  113.7 0.0 copy-start
  113.7 1.7 copy-done
  115.3 0.0 copy-start.1
  115.3 1.7 copy-done.1
  117.0 0.0 copy-start.2
  117.0 1.0 copy-done.2
  118.0 0.0 copy-start.3
  118.0 1.0 copy-done.3
  119.0 0.0 copy-start.4
  119.0 0.7 copy-done.4
  119.7 0.0 copy-start.5
  119.7 0.7 copy-done.5
  120.4 0.0 copy-start.6
  120.4 0.7 copy-done.6
  121.1 0.0 copy-start.7
  121.1 0.7 copy-done.7
  121.8 0.0 copy-start.8
  121.8 0.7 copy-done.8
  122.4 0.0 copy-start.9
  122.4 0.7 copy-done.9
  123.1 88.2 %block_chain.1 = (f32[49,768]{1,0:T(8,128)S(1)}, f32[1,768]{1,0:T(1,128)S(1)}, f32[1,768]{1,0:T(1,128)S(1)}, f32[1,768]{1,0:T(1,128)S(1)}, f32[1,768]{1,0:T(1,128)S(1)}) custom-call(bf16[4,4,16,768]{3,2,1,0:T(8,128)(2,1)S(1)} %copy-done.2, bf16[4,4,16,768]{3,2,1,0:T(8,128)(2,1)S(1)} %copy-done.3, bf16[768,1536]{1,0:T(8,128)(2,1)S(1)} %bitcast.6, ...), custom_call_target="tpu_custom_call" | custom-call | tf_op jit(solution)/shard_map/block_chain/pallas_call | solution.py:395
  211.3 0.8 copy.16
  212.1 0.6 copy.24
  212.7 0.6 copy.25
  213.3 0.6 copy.26
  213.8 0.6 copy.27
Async XLA Ops:
  7.2 55.6 %all-gather.5.cloned.1.call-start = ((), (), s32[]{:S(2)}) async-start(), calls=%async_computation | async-start | bytes 2949120 | tf_op jit(solution)/shard_map/all_gather | solution.py:391
  7.9 105.8 %all-gather.7.cloned.1.call-start = ((), (), s32[]{:S(2)}) async-start(), calls=%async_computation.1 | async-start | bytes 2949120 | tf_op jit(solution)/shard_map/all_gather | solution.py:392
  113.7 1.7 copy-start
  115.3 1.7 copy-start.1
  117.0 1.0 copy-start.2
  118.0 1.0 copy-start.3
  119.0 0.7 copy-start.4
  119.7 0.7 copy-start.5
  120.4 0.7 copy-start.6
  121.1 0.7 copy-start.7
  121.8 0.7 copy-start.8
  122.4 0.7 copy-start.9
Sparse Core Ops, SparseCore 0:
  9.6 53.1 all-gather.4
  64.4 49.2 all-gather.6

commit v2 on v1

--- a/solution.py
+++ b/solution.py
@@ -30,13 +30,15 @@
 
 
 def chain_kernel(
-    sections, slabs, loss_scale,
+    sections, slabs, copies, gathered, loss_scale,
+    latent_in, target_in, w_expand_in, b_expand_in, w_reduce_in, b_reduce_in,
+    taps_in, offset_in, gain_in, shift_in, scale_in,
+    kernel_out, offset_out, gain_out, shift_out, scale_out,
     latent, target, w_expand, b_expand, w_reduce, b_reduce, taps, offset, gain, shift, scale,
-    kernel_out, offset_out, gain_out, shift_out, scale_out,
     frame, output, normed_s, inverse_s, bend_s, branch_s,
     cot_in, slope_frame, cot, slope_low, slope_s, grid_s, token_s, pad, taps_next,
     kernel_sum, small_sum, slots,
-    fwd_send, edge_send, fwd_recv, bwd_send, bwd_recv, tap_send, tap_recv, sum_send, sum_recv,
+    fwd_send, edge_send, fwd_recv, bwd_send, bwd_recv, tap_send, tap_recv, sum_send, sum_recv, load_sem, part_send, part_recv,
 ):
     sec = lax.axis_index("section")
     row = lax.axis_index("rows")
@@ -47,6 +49,23 @@
     tall = height + 2 * MARGIN
     first, last = sec == 0, sec == sections - 1
     has_low, has_high = row > 0, row < slabs - 1
+
+    group = lax.axis_index("groups")
+
+    def rows_of(whole, shard):
+        depth = whole.shape[0] // slabs
+        return pl.ds(pl.multiple_of(shard * depth, 16), depth)
+
+    local = []
+    for source, dest in (
+        (w_expand_in, w_expand), (w_reduce_in, w_reduce), (taps_in, taps), (latent_in, latent),
+        (target_in, target), (b_expand_in, b_expand), (b_reduce_in, b_reduce),
+        (offset_in, offset), (gain_in, gain), (shift_in, shift), (scale_in, scale),
+    ):
+        if len(local) < 2 and not gathered:
+            dest = dest.at[rows_of(dest, row)]
+        local.append(pltpu.make_async_copy(source, dest, load_sem.at[len(local)]))
+        local[-1].start()
 
     barrier = pltpu.get_barrier_semaphore()
     greeted = jnp.int32(slabs - 1)
@@ -67,7 +86,105 @@
                     device_id={"section": sec + ds, "rows": row + dr}, device_id_type=MESH,
                 )
             greeted = greeted + jnp.where(there, 1, 0)
+    if not gathered:
+        for other in range(copies):
+            @pl.when(group != other)
+            def _(other=other):
+                pl.semaphore_signal(
+                    barrier, inc=1, device_id={"groups": other}, device_id_type=MESH
+                )
+        greeted = greeted + (copies - 1)
     pl.semaphore_wait(barrier, greeted)
+
+    weights = ((w_expand_in, w_expand), (w_reduce_in, w_reduce))
+
+    def part_of(t, shard, part):
+        width = weights[t][1].shape[1] // copies
+        return rows_of(weights[t][1], shard), pl.ds(pl.multiple_of(part * width, LANES), width)
+
+    def along(t, shard, onward, own=False):
+        rows, cols = part_of(t, shard, group)
+        dest = weights[t][1].at[rows, cols]
+        source = weights[t][0].at[:, cols] if own else dest
+        to_row = jnp.minimum(row + 1, slabs - 1) if onward == 0 else jnp.maximum(row - 1, 0)
+        return pltpu.make_async_remote_copy(
+            src_ref=source, dst_ref=dest,
+            send_sem=part_send.at[t, shard, onward], recv_sem=part_recv.at[t, shard, group],
+            device_id={"rows": to_row}, device_id_type=MESH,
+        )
+
+    def across(t, shard, other, arriving=False):
+        part = other if arriving else group
+        block = weights[t][1].at[part_of(t, shard, part)]
+        return pltpu.make_async_remote_copy(
+            src_ref=block, dst_ref=block,
+            send_sem=part_send.at[t, shard, 2 + other], recv_sem=part_recv.at[t, shard, part],
+            device_id={"groups": other}, device_id_type=MESH,
+        )
+
+    def each_other_copy(act):
+        for other in range(copies):
+            @pl.when(group != other)
+            def _(other=other):
+                act(other)
+
+    def start_parts():
+        for t in range(2):
+            @pl.when(row < slabs - 1)
+            def _(t=t):
+                along(t, row, 0, own=True).start()
+
+            @pl.when(row > 0)
+            def _(t=t):
+                along(t, row, 1, own=True).start()
+
+    def pass_parts():
+        for t in range(2):
+            for far in range(1, slabs):
+                @pl.when(row - far >= 0)
+                def _(t=t, far=far):
+                    shard = row - far
+                    along(t, shard, 0).wait_recv()
+
+                    @pl.when(row < slabs - 1)
+                    def _():
+                        along(t, shard, 0).start()
+                    each_other_copy(lambda other: across(t, shard, other).start())
+
+                @pl.when(row + far < slabs)
+                def _(t=t, far=far):
+                    shard = row + far
+                    along(t, shard, 1).wait_recv()
+
+                    @pl.when(row > 0)
+                    def _():
+                        along(t, shard, 1).start()
+                    each_other_copy(lambda other: across(t, shard, other).start())
+        for t in range(2):
+            for shard in range(slabs):
+                @pl.when(row != shard)
+                def _(t=t, shard=shard):
+                    each_other_copy(lambda other: across(t, shard, other, True).wait_recv())
+
+    def finish_parts():
+        for t in range(2):
+            for shard in range(slabs):
+                @pl.when((row >= shard) & (row < slabs - 1))
+                def _(t=t, shard=shard):
+                    along(t, shard, 0).wait_send()
+
+                @pl.when((row <= shard) & (row > 0))
+                def _(t=t, shard=shard):
+                    along(t, shard, 1).wait_send()
+
+                @pl.when(row != shard)
+                def _(t=t, shard=shard):
+                    each_other_copy(lambda other: across(t, shard, other).wait_send())
+
+    if not gathered:
+        start_parts()
+    for copy in local:
+        copy.wait()
 
     def remote(source, dest, send, recv, to_sec, to_row):
         return pltpu.make_async_remote_copy(
@@ -130,6 +247,8 @@
     pad[:, pl.ds(SIDE + breadth, SIDE)] = jnp.zeros((tall, SIDE, channels), jnp.float32)
     kernel_sum[...] = jnp.zeros_like(kernel_sum)
     small_sum[...] = jnp.zeros_like(small_sum)
+    if not gathered:
+        pass_parts()
 
     def lanes_of(c):
         return pl.ds(pl.multiple_of(c * LANES, LANES), LANES)
@@ -324,6 +443,8 @@
     shift_out[...] = total[spots + 2 : spots + 3]
     scale_out[...] = total[spots + 3 : spots + 4]
 
+    if not gathered:
+        finish_parts()
     for other in range(slabs):
         @pl.when(row != other)
         def _(other=other):
@@ -388,17 +509,30 @@
     tall = height + 2 * MARGIN
     spots = KS * KS
     loss_scale = 1.0 / math.sqrt(micro * height * slabs * breadth)
-    w_expand = lax.all_gather(expand_weight[0], "rows", axis=0, tiled=True)
-    w_reduce = lax.all_gather(reduce_weight[0], "rows", axis=0, tiled=True)
+    copies = lax.axis_size("groups")
+    w_expand, w_reduce = expand_weight[0], reduce_weight[0]
+    aligned = all(
+        held.shape[0] % 16 == 0 and held.shape[1] % (LANES * copies) == 0
+        for held in (w_expand, w_reduce)
+    )
+    if not aligned:
+        w_expand = lax.all_gather(w_expand, "rows", axis=0, tiled=True)
+        w_reduce = lax.all_gather(w_reduce, "rows", axis=0, tiled=True)
     low, wide = jnp.bfloat16, jnp.float32
     dma, vmem = pltpu.SemaphoreType.DMA, pltpu.VMEM
     found = pl.pallas_call(
-        functools.partial(chain_kernel, sections, slabs, loss_scale),
+        functools.partial(chain_kernel, sections, slabs, copies, not aligned, loss_scale),
         out_shape=(jax.ShapeDtypeStruct((spots, channels), wide),)
         + (jax.ShapeDtypeStruct((1, channels), wide),) * 4,
-        in_specs=[pl.BlockSpec(memory_space=vmem)] * 11,
+        in_specs=[pl.BlockSpec(memory_space=pltpu.HBM)] * 11,
         out_specs=(pl.BlockSpec(memory_space=vmem),) * 5,
         scratch_shapes=[
+            vmem(latent.shape, low), vmem(target.shape, low),
+            vmem((channels, hidden_units), low), vmem((1, hidden_units), wide),
+            vmem((hidden_units, channels), low), vmem((1, channels), wide),
+            vmem((spots, channels), wide),
+            vmem((1, channels), wide), vmem((1, channels), wide),
+            vmem((1, channels), wide), vmem((1, channels), wide),
             vmem((micro, tall, breadth, channels), low),
             vmem((micro, height, breadth, channels), low),
             vmem((micro, tokens, channels), wide),
@@ -421,6 +555,7 @@
             dma((micro, 4)), dma((micro, 4)),
             dma, dma,
             dma((slabs,)), dma((slabs,)),
+            dma((11,)), dma((2, slabs, 2 + copies)), dma((2, slabs, copies)),
         ],
         compiler_params=pltpu.CompilerParams(
             collective_id=0, has_side_effects=True, vmem_limit_bytes=48 * 1024 * 1024

time: 224 us -> 156 us (0.70)
  waiting for transfers between devices: 105 us -> 0 us
  Pallas kernels: 88.2 us -> 146 us
  between operations: 14.1 us -> 0.75 us
  local copies, waits for them, and re-layouts: 13.5 us -> 8.23 us
    all_gather x2 -> x0, waiting for transfers between devices: 104 us -> none  [the longest x1 53.2 us: per_device(): w_expand = lax.all_gather(expand_weight[0], 'rows', axis=0, tiled=True)]
    pallas_call x1, Pallas kernels: 88.2 us -> 146 us  [per_device(): pl.pallas_call(functools.partial(chain_kernel, sections, slabs, copies, n...]
    unnamed x26, local copies, waits for them, and re-layouts: 13.5 us -> 8.23 us
  transfers between devices with their start and end apart: 2 -> 0, of which waited for: 2 -> 0; matrix products, arithmetic and copies ran while one was open for 0% -> 0% of each run, Pallas kernels for 0% -> 0%
where the time goes in v2:
time: 156 us; the launch traced here: 155 us
  Pallas kernels  146 us (94%)
  local copies, waits for them, and re-layouts  8.23 us (5%)
    pallas_call x1, Pallas kernels, per_device(): pl.pallas_call(functools.partial(chain_kernel, sections, slabs, copies, n...  146 us
    unnamed x26, local copies, waits for them, and re-layouts  8.23 us

profile of v2, /device:TPU:0, one launch (start us, length us, event | category | flops | bytes accessed | tf_op | source)
XLA Modules:
  0.0 154.9 jit_solution(565054540895709352)
XLA Ops:
  0.6 0.0 copy-start.4
  0.6 0.0 copy-start.5
  0.7 0.0 copy-start.6
  0.7 0.0 copy-start.7
  0.7 0.0 copy-start.8
  0.7 0.0 copy-start.9
  0.7 1.0 copy.19
  1.7 0.0 copy-done.4
  1.7 0.0 copy-done.5
  1.7 0.0 copy-done.6
  1.7 0.0 copy-done.7
  1.7 0.0 copy-done.8
  1.7 0.0 copy-done.9
  1.7 0.0 copy-start
  1.7 1.1 copy-done
  2.8 0.0 copy-start.1
  2.8 1.1 copy-done.1
  3.8 0.0 copy-start.2
  3.9 1.0 copy-done.2
  4.8 0.0 copy-start.3
  4.8 1.0 copy-done.3
  5.8 145.9 %block_chain.1 = (f32[49,768]{1,0:T(8,128)S(1)}, f32[1,768]{1,0:T(1,128)S(1)}, f32[1,768]{1,0:T(1,128)S(1)}, f32[1,768]{1,0:T(1,128)S(1)}, f32[1,768]{1,0:T(1,128)S(1)}) custom-call(bf16[4,4,16,768]{3,2,1,0:T(8,128)(2,1)S(1)} %copy-done.2, bf16[4,4,16,768]{3,2,1,0:T(8,128)(2,1)S(1)} %copy-done.3, bf16[192,1536]{1,0:T(8,128)(2,1)S(1)} %bitcast.7, ...), custom_call_target="tpu_custom_call" | custom-call | tf_op jit(solution)/shard_map/block_chain/pallas_call | solution.py:523
  151.8 0.8 copy.16
  152.6 0.6 copy.24
  153.2 0.6 copy.25
  153.8 0.6 copy.26
  154.3 0.6 copy.27
Async XLA Ops:
  0.6 1.0 copy-start.4
  0.6 1.0 copy-start.5
  0.7 1.0 copy-start.6
  0.7 1.0 copy-start.7
  0.7 1.0 copy-start.8
  0.7 1.0 copy-start.9
  1.7 1.1 copy-start
  2.8 1.1 copy-start.1
  3.8 1.0 copy-start.2
  4.8 1.0 copy-start.3

commit v3 on v2

--- a/solution.py
+++ b/solution.py
@@ -37,8 +37,9 @@
     latent, target, w_expand, b_expand, w_reduce, b_reduce, taps, offset, gain, shift, scale,
     frame, output, normed_s, inverse_s, bend_s, branch_s,
     cot_in, slope_frame, cot, slope_low, slope_s, grid_s, token_s, pad, taps_next,
-    kernel_sum, small_sum, slots,
-    fwd_send, edge_send, fwd_recv, bwd_send, bwd_recv, tap_send, tap_recv, sum_send, sum_recv, load_sem, part_send, part_recv,
+    kernel_sum, small_sum, parts, slots, sums,
+    fwd_send, edge_send, fwd_recv, bwd_send, bwd_recv, tap_send, tap_recv, sum_send, sum_recv, whole_send, whole_recv,
+    load_sem, part_send, part_recv,
 ):
     sec = lax.axis_index("section")
     row = lax.axis_index("rows")
@@ -281,7 +282,7 @@
             for b in range(KS):
                 column = columns(b, lanes)
                 for a in range(KS):
-                    summed = summed + taps[pl.ds(KS * a + b, 1), lanes] * column[a : a + height]
+                    summed = summed + taps[KS * a + b, :, lanes] * column[a : a + height]
             grid_s[:, :, lanes] = summed
 
         mixed = grid_s[...].reshape(tokens, channels)
@@ -363,7 +364,7 @@
                         begin = 2 * MARGIN - a
                         summed = (
                             summed
-                            + taps_next[pl.ds(KS * a + b, 1), lanes] * column[begin : begin + height]
+                            + taps_next[KS * a + b, :, lanes] * column[begin : begin + height]
                         )
                 passed = cot_in[m, :, :, lanes].astype(jnp.float32) + summed
                 cot[m, :, :, lanes] = passed.astype(jnp.bfloat16)
@@ -417,38 +418,51 @@
                     kernel_sum[KS * a + b, :, lanes] += eight_rows(term)
 
     spots = KS * KS
-    slots[row, pl.ds(0, spots)] = jnp.sum(kernel_sum[...], axis=1)
-    slots[row, pl.ds(spots, 4)] = jnp.sum(small_sum[...], axis=1)
-
-    def sum_copy(other, send_at, recv_at):
-        return remote(slots.at[row], slots.at[row], sum_send.at[send_at], sum_recv.at[recv_at],
-                      sec, other)
-
-    for other in range(slabs):
-        @pl.when(row != other)
-        def _(other=other):
-            sum_copy(other, other, row).start()
-    for other in range(slabs):
-        @pl.when(row != other)
-        def _(other=other):
-            copy = remote(slots.at[other], slots.at[other], sum_send.at[other],
-                          sum_recv.at[other], sec, other)
-            copy.wait_recv()
+    share = parts.shape[1]
+    for i in range(slabs * share):
+        if i < spots:
+            line = jnp.sum(kernel_sum[i], axis=0, keepdims=True)
+        elif i < spots + 4:
+            line = jnp.sum(small_sum[i - spots], axis=0, keepdims=True)
+        else:
+            line = jnp.zeros((1, channels), jnp.float32)
+        parts[i // share, pl.ds(i % share, 1)] = line
+
+    def sum_copy(other, arriving=False):
+        at = other if arriving else row
+        return remote(parts.at[other], slots.at[at], sum_send.at[other], sum_recv.at[at], sec, other)
+
+    def whole_copy(other, arriving=False):
+        at = other if arriving else row
+        return remote(sums.at[at], sums.at[at], whole_send.at[other], whole_recv.at[at], sec, other)
+
+    def each_other_slab(act):
+        for other in range(slabs):
+            @pl.when(row != other)
+            def _(other=other):
+                act(other)
+
+    each_other_slab(lambda other: sum_copy(other).start())
+    slots[row] = parts[row]
+    each_other_slab(lambda other: sum_copy(other, True).wait_recv())
     total = slots[0]
     for other in range(1, slabs):
         total = total + slots[other]
-    kernel_out[...] = total[:spots]
-    offset_out[...] = total[spots : spots + 1]
-    gain_out[...] = total[spots + 1 : spots + 2]
-    shift_out[...] = total[spots + 2 : spots + 3]
-    scale_out[...] = total[spots + 3 : spots + 4]
+    sums[row] = total
+    each_other_slab(lambda other: whole_copy(other).start())
+    each_other_slab(lambda other: whole_copy(other, True).wait_recv())
+    small_outs = (offset_out, gain_out, shift_out, scale_out)
+    for i in range(spots + 4):
+        line = sums[i // share, pl.ds(i % share, 1)]
+        if i < spots:
+            kernel_out[i] = line
+        else:
+            small_outs[i - spots][...] = line
 
     if not gathered:
         finish_parts()
-    for other in range(slabs):
-        @pl.when(row != other)
-        def _(other=other):
-            sum_copy(other, other, row).wait_send()
+    each_other_slab(lambda other: sum_copy(other).wait_send())
+    each_other_slab(lambda other: whole_copy(other).wait_send())
 
     @pl.when(sec > 0)
     def _():
@@ -508,6 +522,7 @@
     tokens = height * breadth
     tall = height + 2 * MARGIN
     spots = KS * KS
+    share = -(-(spots + 4) // slabs)
     loss_scale = 1.0 / math.sqrt(micro * height * slabs * breadth)
     copies = lax.axis_size("groups")
     w_expand, w_reduce = expand_weight[0], reduce_weight[0]
@@ -522,7 +537,7 @@
     dma, vmem = pltpu.SemaphoreType.DMA, pltpu.VMEM
     found = pl.pallas_call(
         functools.partial(chain_kernel, sections, slabs, copies, not aligned, loss_scale),
-        out_shape=(jax.ShapeDtypeStruct((spots, channels), wide),)
+        out_shape=(jax.ShapeDtypeStruct((spots, 1, channels), wide),)
         + (jax.ShapeDtypeStruct((1, channels), wide),) * 4,
         in_specs=[pl.BlockSpec(memory_space=pltpu.HBM)] * 11,
         out_specs=(pl.BlockSpec(memory_space=vmem),) * 5,
@@ -530,7 +545,7 @@
             vmem(latent.shape, low), vmem(target.shape, low),
             vmem((channels, hidden_units), low), vmem((1, hidden_units), wide),
             vmem((hidden_units, channels), low), vmem((1, channels), wide),
-            vmem((spots, channels), wide),
+            vmem((spots, 1, channels), wide),
             vmem((1, channels), wide), vmem((1, channels), wide),
             vmem((1, channels), wide), vmem((1, channels), wide),
             vmem((micro, tall, breadth, channels), low),
@@ -547,25 +562,27 @@
             vmem((height, breadth, channels), wide),
             vmem((tokens, channels), wide),
             vmem((tall, breadth + 2 * SIDE, channels), wide),
-            vmem((spots, channels), wide),
+            vmem((spots, 1, channels), wide),
             vmem((spots, 8, channels), wide),
             vmem((4, 8, channels), wide),
-            vmem((slabs, spots + 4, channels), wide),
+            vmem((slabs, share, channels), wide),
+            vmem((slabs, share, channels), wide),
+            vmem((slabs, share, channels), wide),
             dma((micro, 3)), dma((micro, 3)), dma((micro, 3)),
             dma((micro, 4)), dma((micro, 4)),
             dma, dma,
-            dma((slabs,)), dma((slabs,)),
+            dma((slabs,)), dma((slabs,)), dma((slabs,)), dma((slabs,)),
             dma((11,)), dma((2, slabs, 2 + copies)), dma((2, slabs, copies)),
         ],
         compiler_params=pltpu.CompilerParams(
-            collective_id=0, has_side_effects=True, vmem_limit_bytes=48 * 1024 * 1024
+            collective_id=0, has_side_effects=True, vmem_limit_bytes=62 * 1024 * 1024
         ),
         name="block_chain",
     )(
         latent, target, w_expand, expand_bias, w_reduce, reduce_bias,
-        depth_kernel[0], depth_offset, norm_gain, norm_shift, layer_scale,
+        depth_kernel.transpose(1, 0, 2), depth_offset, norm_gain, norm_shift, layer_scale,
     )
-    return (found[0][None],) + tuple(found[1:])
+    return (found[0].transpose(1, 0, 2),) + tuple(found[1:])
 
 
 def solution(mesh):

time: 156 us -> 151 us (0.968)
  local copies, waits for them, and re-layouts: 8.23 us -> 4.2 us
    unnamed x26 -> x13, local copies, waits for them, and re-layouts: 8.23 us -> 4.2 us
where the time goes in v3:
time: 151 us
  Pallas kernels  146 us (97%)
  local copies, waits for them, and re-layouts  4.2 us (3%)
    pallas_call x1, Pallas kernels, per_device(): pl.pallas_call(functools.partial(chain_kernel, sections, slabs, copies, n...  146 us
    unnamed x13, local copies, waits for them, and re-layouts  4.2 us

profile of v3, /device:TPU:0, one launch (start us, length us, event | category | flops | bytes accessed | tf_op | source)
XLA Modules:
  0.0 150.8 jit_solution(7562403812226995894)
XLA Ops:
  0.6 146.0 %block_chain.1 = (f32[49,1,768]{2,1,0:T(1,128)}, f32[1,768]{1,0:T(1,128)}, f32[1,768]{1,0:T(1,128)}, f32[1,768]{1,0:T(1,128)}, f32[1,768]{1,0:T(1,128)}) custom-call(bf16[4,4,16,768]{3,2,1,0:T(8,128)(2,1)} %latent_in.1, bf16[4,4,16,768]{3,2,1,0:T(8,128)(2,1)} %target_in.1, bf16[192,1536]{1,0:T(8,128)(2,1)} %bitcast.4, f32[1,1536]{1,0:T(1,128)} %b_expand_in.1, ...), custom_call_target="tpu_custom_call" | custom-call | tf_op jit(solution)/shard_map/block_chain/pallas_call | solution.py:538
  146.6 0.0 copy-start.3
  146.6 1.6 %copy.21 = f32[1,49,768]{2,0,1:T(1,128)} copy(f32[1,49,768]{2,0,1:T(1,128)} %bitcast.6) | data formatting | bytes 301056
  148.2 0.0 copy-done.3
  148.2 0.0 copy-start.2
  148.2 0.6 copy.22
  148.8 0.1 copy-done.2
  148.9 0.0 copy-start.1
  148.9 0.6 copy.23
  149.5 0.1 copy-done.1
  149.6 0.0 copy-start
  149.6 0.6 copy.24
  150.1 0.1 copy-done
  150.2 0.6 copy.25
Async XLA Ops:
  146.6 1.6 %copy-start.3 = (f32[1,768]{1,0:T(1,128)S(1)}, f32[1,768]{1,0:T(1,128)}, u32[]{:S(2)}) copy-start(f32[1,768]{1,0:T(1,128)} %get-tuple-element.21) | copy-start | bytes 9220
  148.2 0.7 copy-start.2
  148.9 0.7 copy-start.1
  149.6 0.7 copy-start

commit v4 on v3

--- a/solution.py
+++ b/solution.py
@@ -16,6 +16,7 @@
 SQRT_HALF = 0.7071067811865476
 INV_ROOT_TAU = 0.3989422804014327
 MESH = pl.DeviceIdType.MESH
+CUTS = 4
 
 
 def contract_last(left, right):
@@ -97,16 +98,21 @@
         greeted = greeted + (copies - 1)
     pl.semaphore_wait(barrier, greeted)
 
-    weights = ((w_expand_in, w_expand), (w_reduce_in, w_reduce))
+    weights = ((w_expand_in, w_expand),) * CUTS + ((w_reduce_in, w_reduce),) * CUTS
 
     def part_of(t, shard, part):
-        width = weights[t][1].shape[1] // copies
-        return rows_of(weights[t][1], shard), pl.ds(pl.multiple_of(part * width, LANES), width)
+        whole = weights[t][1]
+        depth, width = whole.shape[0] // slabs, whole.shape[1] // copies
+        begin = shard * depth + (t % CUTS) * (depth // CUTS)
+        return (
+            pl.ds(pl.multiple_of(begin, 16), depth // CUTS),
+            pl.ds(pl.multiple_of(part * width, LANES), width),
+        )
 
     def along(t, shard, onward, own=False):
         rows, cols = part_of(t, shard, group)
         dest = weights[t][1].at[rows, cols]
-        source = weights[t][0].at[:, cols] if own else dest
+        source = weights[t][0].at[part_of(t, 0, group)] if own else dest
         to_row = jnp.minimum(row + 1, slabs - 1) if onward == 0 else jnp.maximum(row - 1, 0)
         return pltpu.make_async_remote_copy(
             src_ref=source, dst_ref=dest,
@@ -130,7 +136,7 @@
                 act(other)
 
     def start_parts():
-        for t in range(2):
+        for t in range(2 * CUTS):
             @pl.when(row < slabs - 1)
             def _(t=t):
                 along(t, row, 0, own=True).start()
@@ -140,7 +146,7 @@
                 along(t, row, 1, own=True).start()
 
     def pass_parts():
-        for t in range(2):
+        for t in range(2 * CUTS):
             for far in range(1, slabs):
                 @pl.when(row - far >= 0)
                 def _(t=t, far=far):
@@ -161,14 +167,14 @@
                     def _():
                         along(t, shard, 1).start()
                     each_other_copy(lambda other: across(t, shard, other).start())
-        for t in range(2):
+        for t in range(2 * CUTS):
             for shard in range(slabs):
                 @pl.when(row != shard)
                 def _(t=t, shard=shard):
                     each_other_copy(lambda other: across(t, shard, other, True).wait_recv())
 
     def finish_parts():
-        for t in range(2):
+        for t in range(2 * CUTS):
             for shard in range(slabs):
                 @pl.when((row >= shard) & (row < slabs - 1))
                 def _(t=t, shard=shard):
@@ -527,7 +533,7 @@
     copies = lax.axis_size("groups")
     w_expand, w_reduce = expand_weight[0], reduce_weight[0]
     aligned = all(
-        held.shape[0] % 16 == 0 and held.shape[1] % (LANES * copies) == 0
+        held.shape[0] % (16 * CUTS) == 0 and held.shape[1] % (LANES * copies) == 0
         for held in (w_expand, w_reduce)
     )
     if not aligned:
@@ -572,7 +578,8 @@
             dma((micro, 4)), dma((micro, 4)),
             dma, dma,
             dma((slabs,)), dma((slabs,)), dma((slabs,)), dma((slabs,)),
-            dma((11,)), dma((2, slabs, 2 + copies)), dma((2, slabs, copies)),
+            dma((11,)), dma((2 * CUTS, slabs, 2 + copies)),
+            dma((2 * CUTS, slabs, copies)),
         ],
         compiler_params=pltpu.CompilerParams(
             collective_id=0, has_side_effects=True, vmem_limit_bytes=62 * 1024 * 1024

time: 151 us -> 154 us (1.020)
  Pallas kernels: 146 us -> 149 us
    pallas_call x1, Pallas kernels: 146 us -> 149 us  [per_device(): pl.pallas_call(functools.partial(chain_kernel, sections, slabs, copies, n...]
where the time goes in v4:
time: 154 us; the launch traced here: 153 us
  Pallas kernels  149 us (97%)
  local copies, waits for them, and re-layouts  4.2 us (3%)
    pallas_call x1, Pallas kernels, per_device(): pl.pallas_call(functools.partial(chain_kernel, sections, slabs, copies, n...  149 us
    unnamed x13, local copies, waits for them, and re-layouts  4.2 us

profile of v4, /device:TPU:0, one launch (start us, length us, event | category | flops | bytes accessed | tf_op | source)
XLA Modules:
  0.0 153.4 jit_solution(3954173376737124374)
XLA Ops:
  0.6 148.6 %block_chain.1 = (f32[49,1,768]{2,1,0:T(1,128)}, f32[1,768]{1,0:T(1,128)}, f32[1,768]{1,0:T(1,128)}, f32[1,768]{1,0:T(1,128)}, f32[1,768]{1,0:T(1,128)}) custom-call(bf16[4,4,16,768]{3,2,1,0:T(8,128)(2,1)} %latent_in.1, bf16[4,4,16,768]{3,2,1,0:T(8,128)(2,1)} %target_in.1, bf16[192,1536]{1,0:T(8,128)(2,1)} %bitcast.4, f32[1,1536]{1,0:T(1,128)} %b_expand_in.1, ...), custom_call_target="tpu_custom_call" | custom-call | tf_op jit(solution)/shard_map/block_chain/pallas_call | solution.py:544
  149.2 0.0 copy-start.3
  149.2 1.6 %copy.21 = f32[1,49,768]{2,0,1:T(1,128)} copy(f32[1,49,768]{2,0,1:T(1,128)} %bitcast.6) | data formatting | bytes 301056
  150.8 0.0 copy-done.3
  150.8 0.0 copy-start.2
  150.8 0.6 copy.22
  151.4 0.1 copy-done.2
  151.5 0.0 copy-start.1
  151.5 0.6 copy.23
  152.1 0.1 copy-done.1
  152.2 0.0 copy-start
  152.2 0.6 copy.24
  152.7 0.1 copy-done
  152.8 0.6 copy.25
Async XLA Ops:
  149.2 1.6 %copy-start.3 = (f32[1,768]{1,0:T(1,128)S(1)}, f32[1,768]{1,0:T(1,128)}, u32[]{:S(2)}) copy-start(f32[1,768]{1,0:T(1,128)} %get-tuple-element.21) | copy-start | bytes 9220
  150.8 0.7 copy-start.2
  151.5 0.7 copy-start.1
  152.2 0.7 copy-start

commit v5 on v3

--- a/solution.py
+++ b/solution.py
@@ -161,11 +161,14 @@
                     def _():
                         along(t, shard, 1).start()
                     each_other_copy(lambda other: across(t, shard, other).start())
-        for t in range(2):
-            for shard in range(slabs):
-                @pl.when(row != shard)
-                def _(t=t, shard=shard):
-                    each_other_copy(lambda other: across(t, shard, other, True).wait_recv())
+
+    def take_parts(t, m):
+        if gathered:
+            return
+        for shard in range(slabs):
+            @pl.when((m == 0) & (row != shard))
+            def _(shard=shard):
+                each_other_copy(lambda other: across(t, shard, other, True).wait_recv())
 
     def finish_parts():
         for t in range(2):
@@ -294,6 +297,7 @@
         inverse_s[m] = jnp.broadcast_to(inverse, (tokens, LANES))
         inputs = (normed * gain[...] + shift[...]).astype(jnp.bfloat16)
         branch = jnp.zeros((tokens, channels), jnp.float32) + b_reduce[...]
+        take_parts(0, m)
         for f in range(hidden_units // piece):
             units = pl.ds(f * piece, piece)
             hidden = (
@@ -303,6 +307,8 @@
             below = 0.5 * (1.0 + lax.erf(hidden * SQRT_HALF))
             bend_s[m, :, units] = below + hidden * jnp.exp(-0.5 * hidden * hidden) * INV_ROOT_TAU
             active = (hidden * below).astype(jnp.bfloat16)
+            if f == 0:
+                take_parts(1, m)
             branch = branch + jnp.dot(active, w_reduce[units, :], preferred_element_type=jnp.float32)
         branch_s[m] = branch
         source = frame[m, pl.ds(MARGIN, height)].astype(jnp.float32)

time: 151 us -> 150 us (level)
  no operation moved by 1% of the time
where the time goes in v5:
time: 150 us; the launch traced here: 149 us
  Pallas kernels  145 us (97%)
  local copies, waits for them, and re-layouts  4.2 us (3%)
    pallas_call x1, Pallas kernels, per_device(): pl.pallas_call(functools.partial(chain_kernel, sections, slabs, copies, n...  145 us
    unnamed x13, local copies, waits for them, and re-layouts  4.2 us

profile of v5, /device:TPU:0, one launch (start us, length us, event | category | flops | bytes accessed | tf_op | source)
XLA Modules:
  0.0 149.4 jit_solution(4621743102133055008)
XLA Ops:
  0.6 144.6 %block_chain.1 = (f32[49,1,768]{2,1,0:T(1,128)}, f32[1,768]{1,0:T(1,128)}, f32[1,768]{1,0:T(1,128)}, f32[1,768]{1,0:T(1,128)}, f32[1,768]{1,0:T(1,128)}) custom-call(bf16[4,4,16,768]{3,2,1,0:T(8,128)(2,1)} %latent_in.1, bf16[4,4,16,768]{3,2,1,0:T(8,128)(2,1)} %target_in.1, bf16[192,1536]{1,0:T(8,128)(2,1)} %bitcast.4, f32[1,1536]{1,0:T(1,128)} %b_expand_in.1, ...), custom_call_target="tpu_custom_call" | custom-call | tf_op jit(solution)/shard_map/block_chain/pallas_call | solution.py:544
  145.2 0.0 copy-start.3
  145.2 1.6 %copy.21 = f32[1,49,768]{2,0,1:T(1,128)} copy(f32[1,49,768]{2,0,1:T(1,128)} %bitcast.6) | data formatting | bytes 301056
  146.8 0.0 copy-done.3
  146.8 0.0 copy-start.2
  146.8 0.6 copy.22
  147.4 0.1 copy-done.2
  147.5 0.0 copy-start.1
  147.5 0.6 copy.23
  148.1 0.1 copy-done.1
  148.2 0.0 copy-start
  148.2 0.6 copy.24
  148.7 0.1 copy-done
  148.8 0.6 copy.25
Async XLA Ops:
  145.2 1.6 %copy-start.3 = (f32[1,768]{1,0:T(1,128)S(1)}, f32[1,768]{1,0:T(1,128)}, u32[]{:S(2)}) copy-start(f32[1,768]{1,0:T(1,128)} %get-tuple-element.21) | copy-start | bytes 9220
  146.8 0.7 copy-start.2
  147.5 0.7 copy-start.1
  148.2 0.7 copy-start
